TPU v7x, 256 devices: a whole 4x4x8 slice. The times are simulated.
256 devices in a mesh: dp: 16 (over x, y), expert: 16 (over z, core).
Axes of the slice: x: 4, y: 4, z: 8, core: 2. Of those that a mesh axis runs over, the one named last changes fastest.
Arguments:
- tokens: bfloat16 [16384, 2048], P(('dp', 'expert')), may hold values from -6 to 6
- cotangent: bfloat16 [16384, 2048], P(('dp', 'expert')), may hold values from -6 to 6
- expert_ids: int32 [16384, 8], P(('dp', 'expert')), may hold values from 0 to 15, all different within a row
- gate_probs: float32 [16384, 8], P(('dp', 'expert')), may hold values from 0.05 to 0.5
- held_before: int32 [16], replicated, may hold values from 0 to 15, each once
- swap_flags: int32 [8], replicated, may hold values from 0 to 1, as said below
- weights: bfloat16 [16, 2048, 3, 384], P('expert'), may hold values from -0.125 to 0.125
Outputs:
- mixed: bfloat16 [16384, 2048], P(('dp', 'expert'))
- token_grads: bfloat16 [16384, 2048], P(('dp', 'expert'))
- gate_grads: float32 [16384, 8], P(('dp', 'expert'))
- weight_grads: float32 [16, 2048, 3, 384], P('expert', 'dp')
Inputs may be any that keep to these rules, and one draw needn't show every extreme that they name: `expert_ids`: each row names 8 different experts. `held_before`: each expert once. `swap_flags`: entry 0 is always 1; the others are 0 or 1.
All inputs are finite; a program needn't handle non-finite values.
Results may differ from a plain program's by a relative error of at most 0.013.
Values may be sent and summed in bfloat16 or wider, within the bound.
A program may use at most 64 MiB of HBM per device.

v0:
```python
import jax
import jax.numpy as jnp
from jax import lax
from jax.sharding import Mesh
from jax.sharding import PartitionSpec as P

DP = ("dp_0", "dp_1")
DP_EXPERT = ("dp_0", "dp_1", "expert")


def in_blocks(x, dim, devices):
    dims = x.shape
    tiles = x.reshape(*dims[:dim], devices, dims[dim] // devices, *dims[dim + 1 :])
    return jnp.moveaxis(tiles, dim, 0)


def cut_rows(length, count):
    lap = length // count
    if lap >= 8:
        lap -= lap % 8
    return [lap * k for k in range(1, count)]


def laid_out(tiles, dim):
    tiles = jnp.moveaxis(tiles, 0, dim)
    dims = tiles.shape
    return tiles.reshape(*dims[:dim], dims[dim] * dims[dim + 1], *dims[dim + 2 :])


def several_exchanges(x, axis, pieces, split_dim, concat_dim):
    tiles = in_blocks(x, split_dim, lax.axis_size(axis))
    widest = max(range(1, max(2, tiles.ndim - 1)), key=lambda d: tiles.shape[d])
    outs = []
    for piece in jnp.split(tiles, cut_rows(tiles.shape[widest], pieces), axis=widest):
        if piece.size:
            outs.append(lax.all_to_all(piece, axis, split_axis=0, concat_axis=0, tiled=True))
    return laid_out(jnp.concatenate(outs, axis=widest), concat_dim)


def summed_rows(terms, axes):
    total = terms.astype(jnp.bfloat16)
    for axis in axes:
        total = lax.psum_scatter(total, axis, scatter_dimension=0, tiled=True)
    return total.astype(jnp.float32)


def swapped(x, axis, bit):
    return lax.ppermute(x, axis, [(i, i ^ 1 << bit) for i in range(lax.axis_size(axis))])


def silu_terms(gate):
    sigma = jax.nn.sigmoid(gate)
    return (gate * sigma, sigma * (1.0 + gate * (1.0 - sigma)))


def on_device(tokens, cotangent, expert_ids, gate_probs, held_before, swap_flags, weights):
    width = tokens.shape[1]
    token_count = tokens.shape[0]
    top_count = expert_ids.shape[1]
    axis_count = lax.axis_size("expert")
    capacity = token_count * top_count // axis_count
    half_axis = axis_count // 2
    pair_bit = axis_count.bit_length() - 2
    own_index = lax.axis_index("expert")
    labels = jnp.arange(axis_count, dtype=jnp.int32)
    moved = swap_flags[own_index % half_axis] == 1
    local_w = weights[0]
    owner_table = jnp.sum(
        (held_before[None, :] == labels[:, None]).astype(jnp.int32) * labels[None, :], axis=1
    )
    hidden_width = local_w.shape[2]
    w_in = local_w[:, :2, :].reshape(width, 2 * hidden_width)
    w_out = local_w[:, 2, :]
    onehot = (expert_ids[:, :, None] == labels[None, None, :]).astype(jnp.int32)
    per_token = jnp.sum(onehot, axis=1)
    earlier = jnp.cumsum(per_token, axis=0) - per_token
    rank = jnp.sum(onehot * earlier[:, None, :], axis=2)
    owner = jnp.sum(onehot * owner_table[None, None, :], axis=2)
    total_slots = axis_count * capacity
    flat_slot = jnp.where(rank < capacity, owner * capacity + rank, total_slots).reshape(-1)
    send = (
        jnp.zeros((total_slots, width), jnp.bfloat16)
        .at[flat_slot]
        .set(jnp.repeat(tokens, top_count, axis=0), mode="drop")
    )
    send = send.reshape(axis_count, capacity, width)
    received = lax.all_to_all(send, "expert", split_axis=0, concat_axis=0, tiled=True)
    row_block = received.reshape(-1, width)
    gate_up = jnp.dot(row_block, w_in, preferred_element_type=jnp.float32)
    silu_value, slope = silu_terms(gate_up[:, :hidden_width])
    forward_hidden = (silu_value * gate_up[:, hidden_width:]).astype(jnp.bfloat16)
    outputs = lax.dot_general(
        forward_hidden, w_out, (((1,), (1,)), ((), ())), preferred_element_type=jnp.float32
    ).astype(jnp.bfloat16)
    returned = several_exchanges(outputs.reshape(received.shape), "expert", 2, 0, 0)
    returned, kept_rows, kept_gate_up = (
        returned,
        received,
        gate_up.reshape(received.shape[0], received.shape[1], 2 * hidden_width),
    )
    picked = (
        returned.reshape(-1, width)
        .at[flat_slot]
        .get(mode="fill", fill_value=0)
        .reshape(token_count, top_count, width)
        .astype(jnp.float32)
    )
    mixed = jnp.sum(gate_probs[:, :, None] * picked, axis=1).astype(jnp.bfloat16)
    cot_wide = cotangent.astype(jnp.float32)
    gate_grads = jnp.einsum("tkd,td->tk", picked, cot_wide)
    weighted = (
        (gate_probs[:, :, None] * cot_wide[:, None, :]).astype(jnp.bfloat16).reshape(-1, width)
    )
    grad_send = (
        jnp.zeros((total_slots, width), jnp.bfloat16).at[flat_slot].set(weighted, mode="drop")
    )
    upstream = lax.all_to_all(
        grad_send.reshape(axis_count, capacity, width),
        "expert",
        split_axis=0,
        concat_axis=0,
        tiled=True,
    ).reshape(-1, width)
    x_rows = kept_rows.reshape(-1, width)
    gate_up = kept_gate_up.reshape(-1, 2 * hidden_width)
    up_part = gate_up[:, hidden_width:]
    silu_value, slope = silu_terms(gate_up[:, :hidden_width])
    hidden = (silu_value * up_part).astype(jnp.bfloat16)
    d_hidden = jnp.dot(upstream, w_out, preferred_element_type=jnp.float32)
    d_gate = (d_hidden * up_part * slope).astype(jnp.bfloat16)
    d_up = (d_hidden * silu_value).astype(jnp.bfloat16)
    back = lax.dot_general(
        jnp.concatenate([d_gate, d_up], axis=1),
        w_in,
        (((1,), (1,)), ((), ())),
        preferred_element_type=jnp.float32,
    ).astype(jnp.bfloat16)
    back_home = lax.all_to_all(
        back.reshape(axis_count, capacity, width), "expert", split_axis=0, concat_axis=0, tiled=True
    ).reshape(-1, width)
    token_grads = jnp.sum(
        back_home.at[flat_slot]
        .get(mode="fill", fill_value=0)
        .reshape(token_count, top_count, width)
        .astype(jnp.float32),
        axis=1,
    ).astype(jnp.bfloat16)
    contract = (((0,), (0,)), ((), ()))
    gate_term = lax.dot_general(x_rows, d_gate, contract, preferred_element_type=jnp.float32)
    up_term = lax.dot_general(x_rows, d_up, contract, preferred_element_type=jnp.float32)
    down_term = lax.dot_general(upstream, hidden, contract, preferred_element_type=jnp.float32)
    share = summed_rows(jnp.stack([gate_term, up_term, down_term], axis=1), DP)
    arrived = swapped(share.astype(jnp.bfloat16), "expert", pair_bit).astype(share.dtype)
    share = jnp.where(moved, arrived, share)
    return (mixed, token_grads, gate_grads, share[None])


def solution(mesh):
    torus = Mesh(mesh.devices.reshape(4, 4, mesh.shape["expert"]), ("dp_0", "dp_1", "expert"))
    in_specs = (
        P(DP_EXPERT, None),
        P(DP_EXPERT, None),
        P(DP_EXPERT, None),
        P(DP_EXPERT, None),
        P(),
        P(),
        P("expert", None, None, None),
    )
    out_specs = (
        P(DP_EXPERT, None),
        P(DP_EXPERT, None),
        P(DP_EXPERT, None),
        P("expert", DP, None, None),
    )
    return jax.shard_map(
        on_device, mesh=torus, in_specs=in_specs, out_specs=out_specs, check_vma=False
    )
```

profile of v0, /device:TPU:2, one launch (start us, length us, event | category | flops | bytes accessed | tf_op | source)
XLA Modules:
  0.0 279.9 jit_solution(10236962615011213378)
XLA Ops:
  7.2 0.8 select_reduce_fusion.2
  8.0 0.7 convert_reduce_fusion
  8.8 0.1 reduce_window_sum.11
  9.0 0.8 select_reduce_fusion
  9.8 0.1 copy.34
  9.8 0.1 select_n.64
  10.0 5.1 %scatter_custom_fusion = bf16[512,2048]{1,0:T(8,128)(2,1)} fusion(s32[512]{0:T(512)S(1)} %bitcast.74, bf16[64,2048]{1,0:T(8,128)(2,1)S(1)} %copy-done, bf16[]{:T(256)} %constant.37.clone.1), kind=kCustom, calls=%fused_computation.21 | custom fusion | bytes 2359298 | tf_op jit(solution)/shard_map/scatter | solution.py:84
  15.1 8.7 %all-to-all-start = ((bf16[16,32,2048]{2,1,0:T(8,128)(2,1)}), bf16[16,32,2048]{2,1,0:T(8,128)(2,1)S(1)}, u32[]{:S(2)}, u32[]{:S(2)}) async-start(bf16[16,32,2048]{2,1,0:T(8,128)(2,1)} %bitcast.2), calls=%async_computation | async-start | bytes 4194304 | tf_op jit(solution)/shard_map/all_to_all | solution.py:87
  23.8 0.1 copy.29
  23.9 0.1 mul.99
  24.0 5.2 %scatter_custom_fusion.1 = bf16[512,2048]{1,0:T(8,128)(2,1)} fusion(s32[512]{0:T(512)S(1)} %bitcast.75, f32[64,2048]{1,0:T(8,128)S(1)} %convert_element_type.48, f32[512]{0:T(512)S(1)} %mul.99, bf16[]{:T(256)} %constant.37.clone.1), kind=kCustom, calls=%fused_computation.16 | custom fusion | flops 2097152 | bytes 2623490 | tf_op jit(solution)/shard_map/scatter | solution.py:115
  29.3 43.7 %all-to-all-done = bf16[16,32,2048]{2,1,0:T(8,128)(2,1)S(1)} async-done(((bf16[16,32,2048]{2,1,0:T(8,128)(2,1)}), bf16[16,32,2048]{2,1,0:T(8,128)(2,1)S(1)}, u32[]{:S(2)}, u32[]{:S(2)}) %all-to-all-start) | async-done | bytes 2097184 | tf_op jit(solution)/shard_map/all_to_all | solution.py:87
  73.0 4.8 %all-to-all-start.3 = ((bf16[16,32,2048]{2,1,0:T(8,128)(2,1)}), bf16[16,32,2048]{2,1,0:T(8,128)(2,1)}, u32[]{:S(2)}, u32[]{:S(2)}) async-start(bf16[16,32,2048]{2,1,0:T(8,128)(2,1)} %bitcast.13), calls=%async_computation.3 | async-start | bytes 4194304 | tf_op jit(solution)/shard_map/all_to_all | solution.py:117
  77.8 0.2 reduce-scatter.3.cloned.1.call-start
  78.0 6.7 %copy.35 = bf16[1,2048,3,384]{1,3,2,0:T(8,128)(2,1)} copy(bf16[1,2048,3,384]{3,1,2,0:T(8,128)(2,1)} %param.13) | data formatting | bytes 9437184 | tf_op args[6]
  84.7 2.3 slice.22
  87.1 1.6 copy-done.2
  88.7 3.0 %fusion.25 = f32[512,768]{1,0:T(8,128)} fusion(bf16[512,2048]{1,0:T(8,128)(2,1)S(1)} %bitcast.69, bf16[2048,768]{0,1:T(8,128)(2,1)S(1)} %bitcast.66), kind=kOutput, calls=%fused_computation.56 | convolution fusion | flops 1610612736 | bytes 6815744 | tf_op jit(solution)/shard_map/dot_general | solution.py:89
  91.7 35.3 %all-to-all-done.3 = bf16[16,32,2048]{2,1,0:T(8,128)(2,1)} async-done(((bf16[16,32,2048]{2,1,0:T(8,128)(2,1)}), bf16[16,32,2048]{2,1,0:T(8,128)(2,1)}, u32[]{:S(2)}, u32[]{:S(2)}) %all-to-all-start.3) | async-done | bytes 2097184 | tf_op jit(solution)/shard_map/all_to_all | solution.py:117
  127.0 3.9 %multiply_convert_fusion.1 = (bf16[512,384]{1,0:T(8,128)(2,1)S(1)}, bf16[512,384]{1,0:T(8,128)(2,1)S(1)}, bf16[512,384]{1,0:T(8,128)(2,1)S(1)}) fusion(f32[512,768]{1,0:T(8,128)} %fusion.25, bf16[512,2048]{1,0:T(8,128)(2,1)} %bitcast.14, bf16[2048,3,384]{0,2,1:T(8,128)(2,1)} %bitcast.64), kind=kOutput, calls=%fused_computation.36 | convolution fusion | flops 808255488 | bytes 6422528 | tf_op jit(solution)/shard_map/dot_general | solution.py:129
  131.0 3.2 %fusion.3 = bf16[2048,1,384]{2,0,1:T(8,128)(2,1)S(1)} fusion(bf16[512,2048]{1,0:T(8,128)(2,1)} %bitcast.14, bf16[512,384]{1,0:T(8,128)(2,1)S(1)} %get-tuple-element.12), kind=kOutput, calls=%fused_computation.15 | convolution fusion | flops 806092800 | bytes 4063232 | tf_op jit(solution)/shard_map/dot_general | solution.py:151
  134.2 1.3 fusion.1
  135.5 1.3 fusion.2
  136.8 2.5 pad_maximum_fusion
  139.3 2.7 convolution_convert_fusion.1
  142.0 1.2 fusion.24
  143.2 31.9 %all_to_all.25 = bf16[16,1,16,2048]{3,2,1,0:T(8,128)(2,1)S(1)} all-to-all(bf16[16,1,16,2048]{3,2,1,0:T(8,128)(2,1)S(1)} %get-tuple-element.10), channel_id=1, replica_groups=mesh['dp_0'=4,'dp_1'=4,'expert'=16] {'expert'}, dimensions={0} | all-to-all | bytes 2097152 | tf_op jit(solution)/shard_map/all_to_all | solution.py:36
  175.1 4.2 %all-to-all-start.2 = ((bf16[16,1,16,2048]{3,2,1,0:T(8,128)(2,1)}), bf16[16,1,16,2048]{3,2,1,0:T(8,128)(2,1)S(1)}, u32[]{:S(2)}, u32[]{:S(2)}) async-start(bf16[16,1,16,2048]{3,2,1,0:T(8,128)(2,1)} %get-tuple-element.11), calls=%async_computation.2 | async-start | bytes 2097152 | tf_op jit(solution)/shard_map/all_to_all | solution.py:36
  179.3 5.0 %convolution_convert_fusion = bf16[512,2048]{1,0:T(8,128)(2,1)} fusion(bf16[2048,768]{0,1:T(8,128)(2,1)} %bitcast.67, bf16[512,384]{1,0:T(8,128)(2,1)S(1)} %copy-done.11, bf16[512,384]{1,0:T(8,128)(2,1)S(1)} %copy-done.9), kind=kOutput, calls=%fused_computation.8 | convolution fusion | flops 1613234176 | bytes 6029312 | tf_op jit(solution)/shard_map/dot_general | solution.py:132
  184.3 21.6 %all-to-all-done.2 = bf16[16,1,16,2048]{3,2,1,0:T(8,128)(2,1)S(1)} async-done(((bf16[16,1,16,2048]{3,2,1,0:T(8,128)(2,1)}), bf16[16,1,16,2048]{3,2,1,0:T(8,128)(2,1)S(1)}, u32[]{:S(2)}, u32[]{:S(2)}) %all-to-all-start.2) | async-done | bytes 1048608 | tf_op jit(solution)/shard_map/all_to_all | solution.py:36
  205.9 1.0 copy-done.1
  206.9 4.8 %all-to-all-start.4 = ((bf16[16,32,2048]{2,1,0:T(8,128)(2,1)}), bf16[16,32,2048]{2,1,0:T(8,128)(2,1)S(1)}, u32[]{:S(2)}, u32[]{:S(2)}) async-start(bf16[16,32,2048]{2,1,0:T(8,128)(2,1)} %bitcast.68), calls=%async_computation.4 | async-start | bytes 4194304 | tf_op jit(solution)/shard_map/all_to_all | solution.py:138
  211.7 0.3 reduce-scatter.5.cloned.1.call-start
  212.0 0.4 reduce-scatter.5.cloned.1.call-update
  212.5 0.1 copy.33
  212.6 0.6 dynamic_slice.3
  213.8 2.7 pad_maximum_fusion.1
  216.6 7.2 %gather_fusion = bf16[512,2048]{1,0:T(8,128)(2,1)} fusion(bf16[512,2048]{1,0:T(8,128)(2,1)} %bitcast.62, s32[1024]{0:T(1024)S(1)} %pad_clamp_fusion), kind=kCustom, calls=%fused_computation | custom fusion | bytes 4196352 | tf_op jit(solution)/shard_map/gather | solution.py:104
  223.8 3.3 %fusion.11 = f32[64,1,8]{2,1,0:T(1,128)S(1)} fusion(bf16[512,2048]{1,0:T(8,128)(2,1)} %gather_fusion, pred[64,8]{1,0:T(8,128)(4,1)S(1)} %copy.33, bf16[64,2048,1]{1,0,2:T(8,128)(2,1)S(1)} %bitcast.73), kind=kOutput, calls=%fused_computation.25 | convolution fusion | flops 3145728 | bytes 2361856 | tf_op jit(solution)/shard_map/tkd,td->tk/dot_general | solution.py:110
  227.1 16.4 %reduce-scatter.5.cloned.1.call-done = bf16[128,3,384]{2,0,1:T(8,128)(2,1)} async-done(((bf16[512,3,384]{2,0,1:T(8,128)(2,1)}), bf16[128,3,384]{2,0,1:T(8,128)(2,1)}) %reduce-scatter.5.cloned.1.call-update) | async-done | bytes 294928 | tf_op jit(solution)/shard_map/reduce_scatter | solution.py:43
  243.5 5.7 %collective-permute-start = (bf16[128,3,384]{2,0,1:T(8,128)(2,1)}, bf16[128,3,384]{2,0,1:T(8,128)(2,1)S(1)}, u32[]{:S(2)}, u32[]{:S(2)}) collective-permute-start(bf16[128,3,384]{2,0,1:T(8,128)(2,1)} %reduce-scatter.5.cloned.1.call-done), channel_id=1, source_target_pairs={{0,8},{1,9},{2,10},{3,11},{4,12},{5,13},{6,14},{7,15},{8,0},{9,1},... | collective-permute-start | bytes 884744 | tf_op jit(solution)/shard_map/ppermute | solution.py:48
  249.2 4.7 %multiply_reduce_fusion = bf16[64,2048]{1,0:T(8,128)(2,1)} fusion(f32[64,8]{1,0:T(8,128)S(1)} %copy.29, bf16[512,2048]{1,0:T(8,128)(2,1)} %gather_fusion, pred[64,8]{1,0:T(8,128)(4,1)S(1)} %copy.33), kind=kLoop, calls=%fused_computation.7 | loop fusion | flops 4063232 | bytes 2361856 | tf_op jit(solution)/shard_map/reduce_sum | solution.py:108
  253.9 0.7 copy.43
  254.5 6.3 %all-to-all-done.4 = bf16[16,32,2048]{2,1,0:T(8,128)(2,1)S(1)} async-done(((bf16[16,32,2048]{2,1,0:T(8,128)(2,1)}), bf16[16,32,2048]{2,1,0:T(8,128)(2,1)S(1)}, u32[]{:S(2)}, u32[]{:S(2)}) %all-to-all-start.4) | async-done | bytes 2097184 | tf_op jit(solution)/shard_map/all_to_all | solution.py:138
  260.9 3.3 %gather_fusion.1 = bf16[512,2048]{1,0:T(8,128)(2,1)} fusion(bf16[512,2048]{1,0:T(8,128)(2,1)S(1)} %bitcast.61, s32[1024]{0:T(1024)S(1)} %pad_clamp_fusion), kind=kCustom, calls=%fused_computation.1 | custom fusion | bytes 4196352 | tf_op jit(solution)/shard_map/gather | solution.py:104
  264.2 3.4 %fusion.6 = bf16[64,2048]{1,0:T(8,128)(2,1)} fusion(bf16[512,2048]{1,0:T(8,128)(2,1)} %gather_fusion.1, pred[64,8]{1,0:T(8,128)(4,1)S(1)} %copy.33), kind=kLoop, calls=%fused_computation.19 | loop fusion | flops 1966080 | bytes 2359808 | tf_op jit(solution)/shard_map/reduce_sum | solution.py:141
  267.6 4.6 %collective-permute-done = bf16[128,3,384]{2,0,1:T(8,128)(2,1)S(1)} collective-permute-done((bf16[128,3,384]{2,0,1:T(8,128)(2,1)}, bf16[128,3,384]{2,0,1:T(8,128)(2,1)S(1)}, u32[]{:S(2)}, u32[]{:S(2)}) %collective-permute-start) | collective-permute-done | bytes 294944 | tf_op jit(solution)/shard_map/ppermute | solution.py:48
  272.2 0.9 select_bitcast_fusion
  (31 shorter events, 0.3 us)
Async XLA Ops:
  7.2 2.8 copy-start
  15.1 8.7 %copy-start.6 = (f32[64,8]{0,1:T(8,128)S(1)}, f32[64,8]{0,1:T(8,128)}, u32[]{:S(2)}) copy-start(f32[64,8]{0,1:T(8,128)} %param.10) | copy-start | bytes 6148
  15.1 8.9 %copy-start.4 = (bf16[64,2048]{1,0:T(8,128)(2,1)S(1)}, bf16[64,2048]{1,0:T(8,128)(2,1)}, u32[]{:S(2)}) copy-start(bf16[64,2048]{1,0:T(8,128)(2,1)} %param.8) | copy-start | bytes 786436
  15.1 57.9 %all-to-all-start = ((bf16[16,32,2048]{2,1,0:T(8,128)(2,1)}), bf16[16,32,2048]{2,1,0:T(8,128)(2,1)S(1)}, u32[]{:S(2)}, u32[]{:S(2)}) async-start(bf16[16,32,2048]{2,1,0:T(8,128)(2,1)} %bitcast.2), calls=%async_computation | async-start | bytes 4194304 | tf_op jit(solution)/shard_map/all_to_all | solution.py:87
  73.0 54.0 %all-to-all-start.3 = ((bf16[16,32,2048]{2,1,0:T(8,128)(2,1)}), bf16[16,32,2048]{2,1,0:T(8,128)(2,1)}, u32[]{:S(2)}, u32[]{:S(2)}) async-start(bf16[16,32,2048]{2,1,0:T(8,128)(2,1)} %bitcast.13), calls=%async_computation.3 | async-start | bytes 4194304 | tf_op jit(solution)/shard_map/all_to_all | solution.py:117
  77.8 134.2 %reduce-scatter.3.cloned.1.call-start = ((), (), s32[]{:S(2)}) async-start(), calls=%async_computation.7 | async-start | bytes 5898240 | tf_op jit(solution)/shard_map/reduce_scatter | solution.py:43
  87.0 1.6 copy-start.2
  130.9 3.2 %copy-start.8 = (bf16[512,384]{1,0:T(8,128)(2,1)}, bf16[512,384]{1,0:T(8,128)(2,1)S(1)}, u32[]{:S(2)}) copy-start(bf16[512,384]{1,0:T(8,128)(2,1)S(1)} %get-tuple-element.8) | copy-start | bytes 1179652
  131.0 4.5 %copy-start.10 = (bf16[512,384]{1,0:T(8,128)(2,1)}, bf16[512,384]{1,0:T(8,128)(2,1)S(1)}, u32[]{:S(2)}) copy-start(bf16[512,384]{1,0:T(8,128)(2,1)S(1)} %get-tuple-element.9) | copy-start | bytes 1179652
  143.2 36.1 %copy-start.9 = (bf16[512,384]{1,0:T(8,128)(2,1)S(1)}, bf16[512,384]{1,0:T(8,128)(2,1)}, u32[]{:S(2)}) copy-start(bf16[512,384]{1,0:T(8,128)(2,1)} %copy-done.8) | copy-start | bytes 1179652
  143.2 36.1 %copy-start.11 = (bf16[512,384]{1,0:T(8,128)(2,1)S(1)}, bf16[512,384]{1,0:T(8,128)(2,1)}, u32[]{:S(2)}) copy-start(bf16[512,384]{1,0:T(8,128)(2,1)} %copy-done.10) | copy-start | bytes 1179652
  175.1 30.8 %all-to-all-start.2 = ((bf16[16,1,16,2048]{3,2,1,0:T(8,128)(2,1)}), bf16[16,1,16,2048]{3,2,1,0:T(8,128)(2,1)S(1)}, u32[]{:S(2)}, u32[]{:S(2)}) async-start(bf16[16,1,16,2048]{3,2,1,0:T(8,128)(2,1)} %get-tuple-element.11), calls=%async_computation.2 | async-start | bytes 2097152 | tf_op jit(solution)/shard_map/all_to_all | solution.py:36
  205.9 1.0 copy-start.1
  205.9 6.7 %copy-start.7 = (s32[8]{0:T(128)S(1)}, s32[8]{0:T(128)}, u32[]{:S(2)}) copy-start(s32[8]{0:T(128)} %param.12) | copy-start | bytes 100
  206.9 54.0 %all-to-all-start.4 = ((bf16[16,32,2048]{2,1,0:T(8,128)(2,1)}), bf16[16,32,2048]{2,1,0:T(8,128)(2,1)S(1)}, u32[]{:S(2)}, u32[]{:S(2)}) async-start(bf16[16,32,2048]{2,1,0:T(8,128)(2,1)} %bitcast.68), calls=%async_computation.4 | async-start | bytes 4194304 | tf_op jit(solution)/shard_map/all_to_all | solution.py:138
  211.7 31.8 %reduce-scatter.5.cloned.1.call-start = ((), (), s32[]{:S(2)}) async-start(), calls=%async_computation.8 | async-start | bytes 1474560 | tf_op jit(solution)/shard_map/reduce_scatter | solution.py:43
  216.6 7.2 %copy-start.5 = (bf16[64,2048]{1,0:T(8,128)(2,1)S(1)}, bf16[64,2048]{1,0:T(8,128)(2,1)}, u32[]{:S(2)}) copy-start(bf16[64,2048]{1,0:T(8,128)(2,1)} %param.8) | copy-start | bytes 786436
  243.5 28.7 %collective-permute-start = (bf16[128,3,384]{2,0,1:T(8,128)(2,1)}, bf16[128,3,384]{2,0,1:T(8,128)(2,1)S(1)}, u32[]{:S(2)}, u32[]{:S(2)}) collective-permute-start(bf16[128,3,384]{2,0,1:T(8,128)(2,1)} %reduce-scatter.5.cloned.1.call-done), channel_id=1, source_target_pairs={{0,8},{1,9},{2,10},{3,11},{4,12},{5,13},{6,14},{7,15},{8,0},{9,1},... | collective-permute-start | bytes 884744 | tf_op jit(solution)/shard_map/ppermute | solution.py:48
  264.2 8.0 %copy-start.3 = (bf16[128,3,384]{2,0,1:T(8,128)(2,1)S(1)}, bf16[128,3,384]{2,0,1:T(8,128)(2,1)}, u32[]{:S(2)}) copy-start(bf16[128,3,384]{2,0,1:T(8,128)(2,1)} %reduce-scatter.5.cloned.1.call-done) | copy-start | bytes 884740
Sparse Core Ops, SparseCore 0:
  139.4 51.4 reduce-scatter.2
  215.1 28.2 reduce-scatter.4
where the time goes:
time: 284 us; the launch traced here: 280 us
  waiting for transfers between devices  128 us (45%)
  blocking collectives  31.9 us (11%)
  local copies, waits for them, and re-layouts  30.4 us (11%)
  starting transfers between devices  28.7 us (10%)
  matrix products  23.7 us (8%)
  other arithmetic  21.9 us (8%)
  between operations  14.9 us (5%)
    all_to_all x1, waiting for transfers between devices, on_device(): lax.all_to_all(send, 'expert', split_axis=0, concat_axis=0, tiled=True)  43.7 us
    all_to_all x1, waiting for transfers between devices, on_device(): lax.all_to_all(grad_send.reshape(axis_count, capacity, width), 'expert',...  35.3 us
    all_to_all x1, blocking collectives, several_exchanges(): lax.all_to_all(piece, axis, split_axis=0, concat_axis=0, tiled=True)  31.9 us
    all_to_all x1, waiting for transfers between devices, several_exchanges(): lax.all_to_all(piece, axis, split_axis=0, concat_axis=0, tiled=True)  21.6 us
    reduce_scatter x2, waiting for transfers between devices, summed_rows(): total = lax.psum_scatter(total, axis, scatter_dimension=0, tiled=True)  16.4 us
    gather x2, local copies, waits for them, and re-layouts, on_device(): picked = returned.reshape(-1, width).at[flat_slot].get(mode='fill', fill_...  10.5 us
    unnamed x26, local copies, waits for them, and re-layouts  9.48 us
    all_to_all x1, starting transfers between devices, on_device(): lax.all_to_all(send, 'expert', split_axis=0, concat_axis=0, tiled=True)  8.7 us
  transfers between devices with their start and end apart: 7, of which 6 were waited for; matrix products, arithmetic and copies ran while one was open for 19% of the time, Pallas kernels for 0%

commit v1 on v0

v1 whole, which is shorter than its diff:
```python
import jax
import jax.numpy as jnp
from jax import lax
from jax.experimental import pallas as pl
from jax.experimental.pallas import tpu as pltpu
from jax.sharding import Mesh
from jax.sharding import PartitionSpec as P

DP = ("dp_0", "dp_1")
DP_EXPERT = ("dp_0", "dp_1", "expert")
MESH = pl.DeviceIdType.MESH
F32, BF16 = jnp.float32, jnp.bfloat16
D, FF, CAP = 2048, 384, 32
TOK, HALF = 64, 32
W3 = 3 * FF
GROUPS = ((0,), (1, 2), (3, 4), (5, 6), (7,))
OFFSETS = (0, -1, 1, -2, 2, -3, 3, 4)
SLOT = {o: s for s, o in enumerate(OFFSETS)}
SLOT[-4] = 7


def row(slot, core, half=0):
    return slot * 128 + core * 64 + half * 32


def kernel(
    hb, flags, ids, probs, tok, cot, w,
    mixed_o, tg_o, gg_o, wg_o,
    xall, call, w_in, w_d, up_slope, silu, hidden, whid, dgu, part_m, part_t, acc_m, acc_t,
    ring_m, ring_t, wg, r1, r2, red, q1, q2, share, relay, arrived,
    wsend, wrecv, wcol, ggsend, ggrecv, kept_ids,
    send_sem, recv_sem, local_sem,
):
    px, py, e = lax.axis_index("dp_0"), lax.axis_index("dp_1"), lax.axis_index("expert")
    pz, pc = lax.div(e, 2), lax.rem(e, 2)

    def index_of(off, other):
        return lax.rem(pz + (off + 8), 8) * 2 + (1 - pc if other else pc)

    def along_z(off, other=0):
        return {"expert": index_of(off, other)}

    def along(axis, step):
        return {axis: lax.rem(lax.axis_index(axis) + (step + 4), 4)}

    copies = {}

    def send(key, src, dst, dev):
        n = len(copies)
        copy = pltpu.make_async_remote_copy(
            src_ref=src, dst_ref=dst, send_sem=send_sem.at[n], recv_sem=recv_sem.at[n],
            device_id=dev, device_id_type=MESH,
        )
        copy.start()
        copies[key] = copy

    def arrive(key):
        copies[key].wait_recv()

    barrier = pltpu.get_barrier_semaphore()
    peers = [along_z(o, r) for o in OFFSETS for r in (0, 1) if (o, r) != (0, 0)]
    peers += [along(a, s) for a in DP for s in (1, -1)]
    for peer in peers:
        pl.semaphore_signal(barrier, inc=1, device_id=peer, device_id_type=MESH)

    local = [
        pltpu.make_async_copy(tok, xall.at[pl.ds(0, TOK)], local_sem.at[0]),
        pltpu.make_async_copy(w.at[0], w_in.at[:, pl.ds(0, FF)], local_sem.at[1]),
        pltpu.make_async_copy(w.at[1], w_in.at[:, pl.ds(FF, FF)], local_sem.at[2]),
        pltpu.make_async_copy(w.at[2], w_d, local_sem.at[3]),
        pltpu.make_async_copy(cot, call.at[pl.ds(0, TOK)], local_sem.at[4]),
    ]
    for copy in local:
        copy.start()
    pl.semaphore_wait(barrier, len(peers))

    def gather_own(name, src, dst):
        for d, h in (("L", 0), ("R", 1), ("L", 1), ("R", 0)):
            step = 1 if d == "L" else -1
            send((name, d, 1, h), src.at[pl.ds(32 * h, 32)],
                 dst.at[pl.ds(row(SLOT[-step], 0, h), 32)], along_z(step))
        send((name, "sib", 0), src, dst.at[pl.ds(64, 64)], along_z(0, 1))

    def gather_step(name, dst, s):
        pieces = [("L", 0), ("R", 1)] + ([("L", 1), ("R", 0)] if s < 4 else [])
        for d, h in pieces:
            step = 1 if d == "L" else -1
            slot = SLOT[-step * s]
            here = dst.at[pl.ds(row(slot, 0, h), 32)]
            arrive((name, d, s, h))
            if s < 3 or (s == 3 and (d, h) in (("L", 0), ("R", 1))):
                there = dst.at[pl.ds(row(SLOT[-step * (s + 1)], 0, h), 32)]
                send((name, d, s + 1, h), here, there, along_z(step))
            send((name, "sib", slot, h), here, dst.at[pl.ds(row(slot, 1, h), 32)], along_z(0, 1))

    def gather_sib(name, slots):
        for slot in slots:
            if slot == 0:
                arrive((name, "sib", 0))
            else:
                for h in (0, 1):
                    arrive((name, "sib", slot, h))

    gather_own("x", tok, xall)

    ids8, p8 = ids[...], probs[...]
    ids2 = jnp.concatenate([ids8, ids8], axis=1)
    p2 = jnp.concatenate([p8, p8], axis=1)
    chosen, prob = [], []
    for s, o in enumerate(OFFSETS):
        for r in (0, 1):
            named = ids2 == hb[index_of(o, r)]
            chosen.append(jnp.sum(jnp.where(named, 1.0, 0.0), axis=0, keepdims=True))
            prob.append(jnp.sum(jnp.where(named, p2, 0.0), axis=0, keepdims=True))
    chosen = jnp.concatenate(chosen, axis=0)
    ri = lax.broadcasted_iota(jnp.int32, (128, 128), 0)
    ci = lax.broadcasted_iota(jnp.int32, (128, 128), 1)
    before = jnp.where((ri < ci) & ((ri < 64) == (ci < 64)), 1.0, 0.0).astype(BF16)
    earlier = jnp.dot(chosen.astype(BF16), before, preferred_element_type=F32)
    kept = jnp.where(earlier < CAP - 0.5, 1.0, 0.0)
    weight = jnp.concatenate(prob, axis=0) * kept
    live = jnp.zeros((8, 128), F32)
    for s, o in enumerate(OFFSETS):
        for r in (0, 1):
            n = 2 * s + r
            named = ids2 == hb[index_of(o, r)]
            live = live + jnp.where(named, jnp.broadcast_to(kept[n : n + 1], (8, 128)), 0.0)
            tile = jnp.broadcast_to(weight[n : n + 1], (8, 128))
            wsend[n] = tile
            if n == 0:
                wrecv[0] = tile
            else:
                send(("w", SLOT[-o], r), wsend.at[n], wrecv.at[2 * SLOT[-o] + r], along_z(o, r))
    kept_ids[...] = jnp.where(live > 0.5, ids2, -1)

    gather_own("c", cot, call)
    for copy in local:
        copy.wait()
    for s in range(8):
        for r in (0, 1):
            if s or r:
                arrive(("w", s, r))
    eye = ri == ci
    for s in range(8):
        both = jnp.where(ci < 64, jnp.broadcast_to(wrecv[2 * s, 0:1, :], (128, 128)),
                         jnp.broadcast_to(wrecv[2 * s + 1, 0:1, :], (128, 128)))
        column = jnp.sum(jnp.where(eye, both, 0.0), axis=1, keepdims=True)
        wcol[pl.ds(s * 128, 128), :] = jnp.broadcast_to(column, (128, 128))

    nt = (((1,), (1,)), ((), ()))

    def forward(g):
        slots = GROUPS[g]
        gather_sib("x", slots)
        rows = pl.ds(slots[0] * 128, 128 * len(slots))
        gate_up = jnp.dot(xall[rows, :], w_in[...], preferred_element_type=F32)
        gate, up = gate_up[:, :FF], gate_up[:, FF:]
        sigma = jax.nn.sigmoid(gate)
        act = gate * sigma
        hid = act * up
        silu[rows, :] = act
        up_slope[rows, :] = up * (sigma * (1.0 + gate * (1.0 - sigma)))
        hidden[rows, :] = hid
        scale = wcol[rows, :]
        wh = (hid * jnp.concatenate([scale] * 3, axis=1)).astype(BF16)
        whid[rows, :] = wh
        part_m[rows, :] = lax.dot_general(wh, w_d[...], nt, preferred_element_type=F32).astype(BF16)
        for s in slots:
            send(("sm", s), part_m.at[pl.ds(row(s, 1), 64)], acc_m.at[pl.ds(64 * s, 64)], along_z(0, 1))

    def backward(g):
        slots = GROUPS[g]
        gather_sib("c", slots)
        rows = pl.ds(slots[0] * 128, 128 * len(slots))
        pulled = jnp.dot(call[rows, :], w_d[...], preferred_element_type=F32)
        inner = jnp.sum(pulled * hidden[rows, :], axis=1, keepdims=True)
        scale = wcol[rows, :]
        dh = pulled * jnp.concatenate([scale] * 3, axis=1)
        dgate = (dh * up_slope[rows, :]).astype(BF16)
        dup = (dh * silu[rows, :]).astype(BF16)
        grads = jnp.concatenate([dgate, dup], axis=1)
        dgu[rows, :] = grads
        part_t[rows, :] = lax.dot_general(grads, w_in[...], nt, preferred_element_type=F32).astype(BF16)
        for n, s in enumerate(slots):
            send(("st", s), part_t.at[pl.ds(row(s, 1), 64)], acc_t.at[pl.ds(64 * s, 64)], along_z(0, 1))
            col = jnp.broadcast_to(inner[128 * n : 128 * n + 128], (128, 128))
            line = jnp.sum(jnp.where(eye, col, 0.0), axis=0, keepdims=True)
            ggsend[s] = jnp.broadcast_to(line, (8, 128))
            o = OFFSETS[s]
            for r in (0, 1):
                if (s, r) == (0, 0):
                    ggrecv[0] = jnp.broadcast_to(line, (8, 128))
                else:
                    send(("g", SLOT[-o], r), ggsend.at[s], ggrecv.at[2 * SLOT[-o] + r], along_z(o, r))

    def pair_sum(name, part, acc, slots):
        for s in slots:
            arrive((name, s))
            a = pl.ds(64 * s, 64)
            acc[a, :] = (acc[a, :].astype(F32) + part[pl.ds(row(s, 0), 64), :].astype(F32)).astype(BF16)

    def ring_send(name, acc, ring, d, k, h, src):
        step = 1 if d == 0 else -1
        send((name, d, k - 1, h), src, ring.at[d, pl.ds(64 * (k - 1) + 32 * h, 32)], along_z(step))

    def ring_start(name, acc, ring):
        for d, k, h in ((0, 4, 0), (1, 4, 1), (0, 3, 1), (1, 3, 0)):
            slot = SLOT[k if d == 0 else -k]
            ring_send(name, acc, ring, d, k, h, acc.at[pl.ds(64 * slot + 32 * h, 32)])

    def ring_step(name, acc, ring, k):
        pieces = [(0, 0), (1, 1)] + ([(0, 1), (1, 0)] if k < 3 else [])
        for d, h in pieces:
            arrive((name, d, k, h))
            slot = SLOT[k if d == 0 else -k]
            there = pl.ds(64 * k + 32 * h, 32)
            mine = acc[pl.ds(64 * slot + 32 * h, 32), :].astype(F32)
            ring[d, there, :] = (ring[d, there, :].astype(F32) + mine).astype(BF16)
            ring_send(name, acc, ring, d, k, h, ring.at[d, there])

    def ring_end(name, acc, ring, out):
        for d in (0, 1):
            for h in (0, 1):
                arrive((name, d, 0, h))
        z64 = pl.ds(0, 64)
        total = acc[z64, :].astype(F32) + ring[0, z64, :].astype(F32) + ring[1, z64, :].astype(F32)
        out[...] = total.astype(BF16)

    tn = (((0,), (0,)), ((), ()))

    def weight_terms(blocks):
        cols = []
        for i, j in blocks:
            place = lax.rem(px + i, 4) * 4 + lax.rem(py + j, 4)
            cols.append(pl.ds(pl.multiple_of(place * 128, 128), 128))
        left = jnp.concatenate([xall[:, c] for c in cols], axis=1)
        out = lax.dot_general(left, dgu[...], tn, preferred_element_type=F32)
        for n, (i, j) in enumerate(blocks):
            wg[i, j, :, pl.ds(0, 2 * FF)] = out[128 * n : 128 * n + 128].astype(BF16)
        left = jnp.concatenate([call[:, c] for c in cols], axis=1)
        out = lax.dot_general(left, whid[...], tn, preferred_element_type=F32)
        for n, (i, j) in enumerate(blocks):
            wg[i, j, :, pl.ds(2 * FF, FF)] = out[128 * n : 128 * n + 128].astype(BF16)

    def wg_at(part, first, second):
        rows = pl.ds(64 * part, 64)
        if part == 0:
            return wg.at[first, second, rows]
        return wg.at[second, first, rows]

    def plane_far(part, d):
        send(("far", part, d), wg_at(part, 2, pl.ds(2 * d, 2)), r2.at[part, d], along(DP[part], 1 - 2 * d))

    def plane_near(part, d):
        second = 2 - 2 * d
        send(("near", part, d), wg_at(part, 1 + 2 * d, pl.ds(second, 2)),
             r1.at[part, d, pl.ds(second, 2)], along(DP[part], 1 - 2 * d))

    def plane_chain(part, d):
        arrive(("far", part, d))
        for n in (0, 1):
            mine = wg_at(part, 1 + 2 * d, 2 * d + n)[...].astype(F32)
            r2[part, d, n] = (r2[part, d, n].astype(F32) + mine).astype(BF16)
        send(("chain", part, d), r2.at[part, d], r1.at[part, d, pl.ds(2 * d, 2)], along(DP[part], 1 - 2 * d))

    def plane_turn(part):
        for d in (0, 1):
            arrive(("near", part, d))
            arrive(("chain", part, d))
        axis = DP[1 - part]
        for n in (2, 1, 3, 0):
            total = wg_at(part, 0, n)[...].astype(F32) + r1[part, 0, n].astype(F32) + r1[part, 1, n].astype(F32)
            red[part, n] = total.astype(BF16)
            if n == 2:
                for d in (0, 1):
                    send(("far2", part, d), red.at[part, 2, pl.ds(32 * d, 32)], q2.at[part, d], along(axis, 1 - 2 * d))
            elif n:
                d = 0 if n == 1 else 1
                other = pl.ds(32 - 32 * d, 32)
                send(("near2", part, d), red.at[part, n, other], q1.at[part, d, other], along(axis, 1 - 2 * d))

    def plane_chain2(part):
        axis = DP[1 - part]
        for d in (0, 1):
            arrive(("far2", part, d))
            these = pl.ds(32 * d, 32)
            mine = red[part, 1 + 2 * d, these, :].astype(F32)
            q2[part, d] = (q2[part, d].astype(F32) + mine).astype(BF16)
            send(("chain2", part, d), q2.at[part, d], q1.at[part, d, these], along(axis, 1 - 2 * d))

    def plane_end(part):
        for d in (0, 1):
            arrive(("near2", part, d))
            arrive(("chain2", part, d))
        total = red[part, 0].astype(F32) + q1[part, 0].astype(F32) + q1[part, 1].astype(F32)
        rows = pl.ds(64 * part, 64)
        share[rows, :] = total.astype(BF16)
        send(("swap", part), share.at[rows], relay.at[rows], along_z(2 - 4 * part))

    def swap_relay(part):
        arrive(("swap", part))
        rows = pl.ds(64 * part, 64)
        send(("swap2", part), relay.at[rows], arrived.at[rows], along_z(2 - 4 * part))

    def swap_end(part):
        arrive(("swap2", part))
        rows = pl.ds(64 * part, 64)
        moved = jnp.full((64, W3), flags[lax.rem(e, 8)], jnp.int32) == 1
        mine = jnp.where(moved, arrived[rows, :].astype(F32), share[rows, :].astype(F32))
        for i in range(3):
            wg_o[i, rows, :] = mine[:, i * FF : (i + 1) * FF]

    mixed = ("m", acc_m, ring_m)
    tgrad = ("t", acc_t, ring_t)

    gather_step("x", xall, 1)
    forward(0)
    gather_step("c", call, 1)
    gather_step("x", xall, 2)
    forward(1)
    backward(0)
    gather_step("c", call, 2)
    gather_step("x", xall, 3)
    forward(2)
    backward(1)
    pair_sum("sm", part_m, acc_m, (0, 1, 2, 3, 4))
    gather_step("c", call, 3)
    gather_step("x", xall, 4)
    forward(4)
    forward(3)
    pair_sum("sm", part_m, acc_m, (7, 5, 6))
    ring_start(*mixed)
    backward(2)
    pair_sum("st", part_t, acc_t, (0, 1, 2, 3, 4))
    gather_step("c", call, 4)
    backward(3)
    backward(4)
    pair_sum("st", part_t, acc_t, (7, 5, 6))
    ring_start(*tgrad)
    ring_step(*mixed, 3)
    weight_terms(((2, 0), (2, 1), (0, 2), (1, 2)))
    plane_far(0, 0)
    plane_far(1, 0)
    ring_step(*tgrad, 3)
    weight_terms(((2, 2), (2, 3), (3, 2), (1, 3)))
    plane_far(0, 1)
    plane_far(1, 1)
    plane_near(0, 0)
    ring_step(*mixed, 2)
    weight_terms(((1, 0), (1, 1), (3, 0), (3, 1)))
    plane_near(0, 1)
    plane_near(1, 0)
    plane_chain(0, 0)
    ring_step(*tgrad, 2)
    weight_terms(((3, 3), (0, 1), (0, 3), (0, 0)))
    plane_near(1, 1)
    plane_chain(1, 0)
    plane_chain(0, 1)
    plane_chain(1, 1)
    ring_step(*mixed, 1)
    ring_step(*tgrad, 1)
    for s in range(8):
        for r in (0, 1):
            if s or r:
                arrive(("g", s, r))
    grads = jnp.zeros((8, 128), F32)
    lane = lax.broadcasted_iota(jnp.int32, (8, 128), 1)
    held = kept_ids[...]
    for s, o in enumerate(OFFSETS):
        for r in (0, 1):
            tile = ggrecv[2 * s + r]
            if r:
                tile = pltpu.roll(tile, 64, 1)
            grads = grads + jnp.where(held == hb[index_of(o, r)], tile, 0.0)
    gg_o[...] = grads[:, :64]
    plane_turn(0)
    plane_turn(1)
    ring_end(*mixed, mixed_o)
    plane_chain2(0)
    plane_chain2(1)
    plane_end(0)
    plane_end(1)
    ring_end(*tgrad, tg_o)
    swap_relay(0)
    swap_relay(1)
    swap_end(0)
    swap_end(1)
    for copy in copies.values():
        copy.wait_send()


COPIES = 240


def on_device(tokens, cotangent, expert_ids, gate_probs, held_before, swap_flags, weights):
    vmem = pl.BlockSpec(memory_space=pltpu.VMEM)
    smem = pl.BlockSpec(memory_space=pltpu.SMEM)
    anywhere = pl.BlockSpec(memory_space=pl.ANY)
    rows = 16 * TOK
    scratch = [
        pltpu.VMEM((rows, D), BF16),
        pltpu.VMEM((rows, D), BF16),
        pltpu.VMEM((D, 2 * FF), BF16),
        pltpu.VMEM((D, FF), BF16),
        pltpu.VMEM((rows, FF), F32),
        pltpu.VMEM((rows, FF), F32),
        pltpu.VMEM((rows, FF), F32),
        pltpu.VMEM((rows, FF), BF16),
        pltpu.VMEM((rows, 2 * FF), BF16),
        pltpu.VMEM((rows, D), BF16),
        pltpu.VMEM((rows, D), BF16),
        pltpu.VMEM((rows // 2, D), BF16),
        pltpu.VMEM((rows // 2, D), BF16),
        pltpu.VMEM((2, 4 * TOK, D), BF16),
        pltpu.VMEM((2, 4 * TOK, D), BF16),
        pltpu.VMEM((4, 4, 128, W3), BF16),
        pltpu.VMEM((2, 2, 4, 64, W3), BF16),
        pltpu.VMEM((2, 2, 2, 64, W3), BF16),
        pltpu.VMEM((2, 4, 64, W3), BF16),
        pltpu.VMEM((2, 2, 64, W3), BF16),
        pltpu.VMEM((2, 2, 32, W3), BF16),
        pltpu.VMEM((128, W3), BF16),
        pltpu.VMEM((128, W3), BF16),
        pltpu.VMEM((128, W3), BF16),
        pltpu.VMEM((16, 8, 128), F32),
        pltpu.VMEM((16, 8, 128), F32),
        pltpu.VMEM((rows, 128), F32),
        pltpu.VMEM((8, 8, 128), F32),
        pltpu.VMEM((16, 8, 128), F32),
        pltpu.VMEM((8, 128), jnp.int32),
        pltpu.SemaphoreType.DMA((COPIES,)),
        pltpu.SemaphoreType.DMA((COPIES,)),
        pltpu.SemaphoreType.DMA((5,)),
    ]
    mixed, token_grads, gate_grads, share = pl.pallas_call(
        kernel,
        out_shape=(
            jax.ShapeDtypeStruct((TOK, D), BF16),
            jax.ShapeDtypeStruct((TOK, D), BF16),
            jax.ShapeDtypeStruct((8, TOK), F32),
            jax.ShapeDtypeStruct((3, 128, FF), F32),
        ),
        in_specs=[smem, smem, vmem, vmem, anywhere, anywhere, anywhere],
        out_specs=(vmem, vmem, vmem, vmem),
        scratch_shapes=scratch,
        compiler_params=pltpu.CompilerParams(
            collective_id=0, has_side_effects=True, vmem_limit_bytes=62 * 1024 * 1024
        ),
    )(
        held_before,
        swap_flags,
        expert_ids.T,
        gate_probs.T,
        tokens,
        cotangent,
        jnp.transpose(weights[0], (1, 0, 2)),
    )
    return mixed, token_grads, gate_grads.T, jnp.transpose(share, (1, 0, 2))[None]


def solution(mesh):
    torus = Mesh(mesh.devices.reshape(4, 4, mesh.shape["expert"]), ("dp_0", "dp_1", "expert"))
    in_specs = (
        P(DP_EXPERT, None),
        P(DP_EXPERT, None),
        P(DP_EXPERT, None),
        P(DP_EXPERT, None),
        P(),
        P(),
        P("expert", None, None, None),
    )
    out_specs = (
        P(DP_EXPERT, None),
        P(DP_EXPERT, None),
        P(DP_EXPERT, None),
        P("expert", DP, None, None),
    )
    return jax.shard_map(
        on_device, mesh=torus, in_specs=in_specs, out_specs=out_specs, check_vma=False
    )
```

time: 284 us -> 131 us (0.46); the launches traced: 280 us -> 131 us
  waiting for transfers between devices: 128 us -> 0 us
  Pallas kernels: 0 us -> 124 us
  blocking collectives: 31.9 us -> 0 us
  starting transfers between devices: 28.7 us -> 0 us
  local copies, waits for them, and re-layouts: 30.4 us -> 6.53 us
  matrix products: 23.7 us -> 0 us
  other arithmetic: 21.9 us -> 0 us
  between operations: 14.9 us -> 0.64 us
    pallas_call x0 -> x1, Pallas kernels: none -> 124 us  [on_device(): pl.pallas_call(kernel, out_shape=(jax.ShapeDtypeStruct((TOK, D), BF16), j...]
    all_to_all x4 -> x0, waiting for transfers between devices: 107 us -> none  [the longest x1 43.7 us: on_device(): lax.all_to_all(send, 'expert', split_axis=0, concat_axis=0, tiled=True)]
    all_to_all x1 -> x0, blocking collectives: 31.9 us -> none  [several_exchanges(): lax.all_to_all(piece, axis, split_axis=0, concat_axis=0, tiled=True)]
    dot_general x8 -> x0, matrix products: 23.7 us -> none  [the longest x1 5.04 us: on_device(): lax.dot_general(jnp.concatenate([d_gate, d_up], axis=1), w_in, (((1,), (1...]
    all_to_all x4 -> x0, starting transfers between devices: 22.5 us -> none  [the longest x1 8.7 us: on_device(): lax.all_to_all(send, 'expert', split_axis=0, concat_axis=0, tiled=True)]
    reduce_scatter x2 -> x0, waiting for transfers between devices: 16.4 us -> none  [summed_rows(): total = lax.psum_scatter(total, axis, scatter_dimension=0, tiled=True)]
    gather x2 -> x0, local copies, waits for them, and re-layouts: 10.5 us -> none  [on_device(): picked = returned.reshape(-1, width).at[flat_slot].get(mode='fill', fill_...]
    reduce_sum x5 -> x0, other arithmetic: 10.4 us -> none  [the longest x1 4.67 us: on_device(): jnp.sum(gate_probs[:, :, None] * picked, axis=1).astype(jnp.bfloat16)]
  transfers between devices with their start and end apart: 7 -> 0, of which waited for: 6 -> 0; matrix products, arithmetic and copies ran while one was open for 19% -> 0% of each run, Pallas kernels for 0% -> 0%
where the time goes in v1:
time: 131 us
  Pallas kernels  124 us (95%)
  local copies, waits for them, and re-layouts  6.53 us (5%)
    pallas_call x1, Pallas kernels, on_device(): pl.pallas_call(kernel, out_shape=(jax.ShapeDtypeStruct((TOK, D), BF16), j...  124 us
    unnamed x4, local copies, waits for them, and re-layouts  6.53 us

profile of v1, /device:TPU:2, one launch (start us, length us, event | category | flops | bytes accessed | tf_op | source)
XLA Modules:
  0.0 131.1 jit_solution(345189578524536665)
XLA Ops:
  0.6 123.9 %shard_map.102 = (bf16[64,2048]{1,0:T(8,128)(2,1)}, bf16[64,2048]{1,0:T(8,128)(2,1)}, f32[8,64]{1,0:T(8,128)}, f32[3,128,384]{2,1,0:T(8,128)}) custom-call(s32[16]{0:T(128)} %hb.1, s32[8]{0:T(128)} %flags.1, s32[8,64]{1,0:T(8,128)} %bitcast.12, f32[8,64]{1,0:T(8,128)} %bitcast.13, bf16[64,2048]{1,0:T(8,128)(2,1)} %tok.1, bf16[64,2048]{1,0:T(8,128)(2,1)} %cot.1, ...), custom_call_target="tpu_custom_call" | custom-call | tf_op jit(solution)/shard_map/pallas_call | solution.py:435
  124.5 1.7 %copy.15 = bf16[64,2048]{1,0:T(8,128)(2,1)} copy(bf16[64,2048]{1,0:T(8,128)(2,1)} %get-tuple-element.16) | data formatting | bytes 524288
  126.2 1.7 %copy.16 = bf16[64,2048]{1,0:T(8,128)(2,1)} copy(bf16[64,2048]{1,0:T(8,128)(2,1)} %get-tuple-element.17) | data formatting | bytes 524288
  127.9 1.3 copy.17
  129.2 1.9 %copy.18 = f32[1,128,3,384]{3,1,2,0:T(8,128)} copy(f32[1,128,3,384]{3,1,2,0:T(8,128)} %bitcast.10) | data formatting | bytes 1179648

commit v2 on v1

--- a/solution.py
+++ b/solution.py
@@ -25,10 +25,10 @@
 
 def kernel(
     hb, flags, ids, probs, tok, cot, w,
-    mixed_o, tg_o, gg_o, wg_o,
+    mixed_h, tg_h, gg_h, wg_h,
     xall, call, w_in, w_d, up_slope, silu, hidden, whid, dgu, part_m, part_t, acc_m, acc_t,
     ring_m, ring_t, wg, r1, r2, red, q1, q2, share, relay, arrived,
-    wsend, wrecv, wcol, ggsend, ggrecv, kept_ids,
+    wall, wcol, ggsend, ggrecv, kept_ids, mixed_o, tg_o, gg_o, wg_o,
     send_sem, recv_sem, local_sem,
 ):
     px, py, e = lax.axis_index("dp_0"), lax.axis_index("dp_1"), lax.axis_index("expert")
@@ -58,7 +58,7 @@
         copies[key].wait_recv()
 
     barrier = pltpu.get_barrier_semaphore()
-    peers = [along_z(o, r) for o in OFFSETS for r in (0, 1) if (o, r) != (0, 0)]
+    peers = [along_z(0, 1), along_z(1), along_z(-1)]
     peers += [along(a, s) for a in DP for s in (1, -1)]
     for peer in peers:
         pl.semaphore_signal(barrier, inc=1, device_id=peer, device_id_type=MESH)
@@ -93,6 +93,21 @@
                 send((name, d, s + 1, h), here, there, along_z(step))
             send((name, "sib", slot, h), here, dst.at[pl.ds(row(slot, 1, h), 32)], along_z(0, 1))
 
+    def weights_own():
+        send(("w", "L", 1), wall.at[0], wall.at[2 * SLOT[-1]], along_z(1))
+        send(("w", "R", 1), wall.at[0], wall.at[2 * SLOT[1]], along_z(-1))
+        send(("w", "sib", 0), wall.at[0], wall.at[1], along_z(0, 1))
+
+    def weights_step(s):
+        for d, step in (("L", 1), ("R", -1)):
+            if (d, s) == ("R", 4):
+                continue
+            slot = SLOT[-step * s]
+            arrive(("w", d, s))
+            if s < (4 if d == "L" else 3):
+                send(("w", d, s + 1), wall.at[2 * slot], wall.at[2 * SLOT[-step * (s + 1)]], along_z(step))
+            send(("w", "sib", slot), wall.at[2 * slot], wall.at[2 * slot + 1], along_z(0, 1))
+
     def gather_sib(name, slots):
         for slot in slots:
             if slot == 0:
@@ -107,50 +122,41 @@
     ids2 = jnp.concatenate([ids8, ids8], axis=1)
     p2 = jnp.concatenate([p8, p8], axis=1)
     chosen, prob = [], []
-    for s, o in enumerate(OFFSETS):
-        for r in (0, 1):
-            named = ids2 == hb[index_of(o, r)]
-            chosen.append(jnp.sum(jnp.where(named, 1.0, 0.0), axis=0, keepdims=True))
-            prob.append(jnp.sum(jnp.where(named, p2, 0.0), axis=0, keepdims=True))
+    for j in range(16):
+        named = ids2 == hb[j]
+        chosen.append(jnp.sum(jnp.where(named, 1.0, 0.0), axis=0, keepdims=True))
+        prob.append(jnp.sum(jnp.where(named, p2, 0.0), axis=0, keepdims=True))
     chosen = jnp.concatenate(chosen, axis=0)
     ri = lax.broadcasted_iota(jnp.int32, (128, 128), 0)
     ci = lax.broadcasted_iota(jnp.int32, (128, 128), 1)
     before = jnp.where((ri < ci) & ((ri < 64) == (ci < 64)), 1.0, 0.0).astype(BF16)
     earlier = jnp.dot(chosen.astype(BF16), before, preferred_element_type=F32)
     kept = jnp.where(earlier < CAP - 0.5, 1.0, 0.0)
-    weight = jnp.concatenate(prob, axis=0) * kept
+    wall[0] = jnp.concatenate(prob, axis=0) * kept
+    weights_own()
+    gather_own("c", cot, call)
     live = jnp.zeros((8, 128), F32)
-    for s, o in enumerate(OFFSETS):
-        for r in (0, 1):
-            n = 2 * s + r
-            named = ids2 == hb[index_of(o, r)]
-            live = live + jnp.where(named, jnp.broadcast_to(kept[n : n + 1], (8, 128)), 0.0)
-            tile = jnp.broadcast_to(weight[n : n + 1], (8, 128))
-            wsend[n] = tile
-            if n == 0:
-                wrecv[0] = tile
-            else:
-                send(("w", SLOT[-o], r), wsend.at[n], wrecv.at[2 * SLOT[-o] + r], along_z(o, r))
+    for j in range(16):
+        live = live + jnp.where(ids2 == hb[j], jnp.broadcast_to(kept[j : j + 1], (8, 128)), 0.0)
     kept_ids[...] = jnp.where(live > 0.5, ids2, -1)
-
-    gather_own("c", cot, call)
     for copy in local:
         copy.wait()
-    for s in range(8):
-        for r in (0, 1):
-            if s or r:
-                arrive(("w", s, r))
     eye = ri == ci
-    for s in range(8):
-        both = jnp.where(ci < 64, jnp.broadcast_to(wrecv[2 * s, 0:1, :], (128, 128)),
-                         jnp.broadcast_to(wrecv[2 * s + 1, 0:1, :], (128, 128)))
-        column = jnp.sum(jnp.where(eye, both, 0.0), axis=1, keepdims=True)
-        wcol[pl.ds(s * 128, 128), :] = jnp.broadcast_to(column, (128, 128))
+
+    def weight_columns(slots):
+        for s in slots:
+            arrive(("w", "sib", s))
+            first = jnp.broadcast_to(wall[2 * s, pl.ds(e, 1), :], (128, 128))
+            second = jnp.broadcast_to(wall[2 * s + 1, pl.ds(e, 1), :], (128, 128))
+            both = jnp.where(ci < 64, first, second)
+            column = jnp.sum(jnp.where(eye, both, 0.0), axis=1, keepdims=True)
+            wcol[pl.ds(s * 128, 128), :] = jnp.broadcast_to(column, (128, 128))
 
     nt = (((1,), (1,)), ((), ()))
 
     def forward(g):
         slots = GROUPS[g]
+        weight_columns(slots)
         gather_sib("x", slots)
         rows = pl.ds(slots[0] * 128, 128 * len(slots))
         gate_up = jnp.dot(xall[rows, :], w_in[...], preferred_element_type=F32)
@@ -228,19 +234,21 @@
 
     tn = (((0,), (0,)), ((), ()))
 
-    def weight_terms(blocks):
+    def weight_terms(blocks, first, count):
+        rows = pl.ds(128 * first, 128 * count)
         cols = []
         for i, j in blocks:
             place = lax.rem(px + i, 4) * 4 + lax.rem(py + j, 4)
             cols.append(pl.ds(pl.multiple_of(place * 128, 128), 128))
-        left = jnp.concatenate([xall[:, c] for c in cols], axis=1)
-        out = lax.dot_general(left, dgu[...], tn, preferred_element_type=F32)
-        for n, (i, j) in enumerate(blocks):
-            wg[i, j, :, pl.ds(0, 2 * FF)] = out[128 * n : 128 * n + 128].astype(BF16)
-        left = jnp.concatenate([call[:, c] for c in cols], axis=1)
-        out = lax.dot_general(left, whid[...], tn, preferred_element_type=F32)
-        for n, (i, j) in enumerate(blocks):
-            wg[i, j, :, pl.ds(2 * FF, FF)] = out[128 * n : 128 * n + 128].astype(BF16)
+        for src, grads, at in ((xall, dgu, 0), (call, whid, 2 * FF)):
+            left = jnp.concatenate([src[rows, c] for c in cols], axis=1)
+            out = lax.dot_general(left, grads[rows, :], tn, preferred_element_type=F32)
+            there = pl.ds(at, out.shape[1])
+            for n, (i, j) in enumerate(blocks):
+                term = out[128 * n : 128 * n + 128]
+                if first:
+                    term = term + wg[i, j, :, there].astype(F32)
+                wg[i, j, :, there] = term.astype(BF16)
 
     def wg_at(part, first, second):
         rows = pl.ds(64 * part, 64)
@@ -312,59 +320,75 @@
 
     mixed = ("m", acc_m, ring_m)
     tgrad = ("t", acc_t, ring_t)
+    blocks = (
+        ((2, 0), (2, 1), (0, 2), (1, 2)),
+        ((2, 2), (2, 3), (3, 2), (1, 3)),
+        ((1, 0), (1, 1), (3, 0), (3, 1)),
+        ((3, 3), (0, 1), (0, 3), (0, 0)),
+    )
+    outs = []
+
+    def put(src, dst):
+        copy = pltpu.make_async_copy(src, dst, local_sem.at[5 + len(outs)])
+        copy.start()
+        outs.append(copy)
 
     gather_step("x", xall, 1)
+    weights_step(1)
     forward(0)
     gather_step("c", call, 1)
     gather_step("x", xall, 2)
+    weights_step(2)
     forward(1)
     backward(0)
+    forward(2)
     gather_step("c", call, 2)
     gather_step("x", xall, 3)
-    forward(2)
+    weights_step(3)
     backward(1)
-    pair_sum("sm", part_m, acc_m, (0, 1, 2, 3, 4))
+    forward(3)
+    backward(2)
+    for some in blocks:
+        weight_terms(some, 0, 3)
+    pair_sum("sm", part_m, acc_m, (0, 1, 2, 3, 4, 5, 6))
     gather_step("c", call, 3)
     gather_step("x", xall, 4)
+    weights_step(4)
+    pair_sum("st", part_t, acc_t, (0, 1, 2, 3, 4))
     forward(4)
-    forward(3)
-    pair_sum("sm", part_m, acc_m, (7, 5, 6))
+    pair_sum("sm", part_m, acc_m, (7,))
     ring_start(*mixed)
-    backward(2)
-    pair_sum("st", part_t, acc_t, (0, 1, 2, 3, 4))
+    backward(3)
+    for some in blocks:
+        weight_terms(some, 3, 4)
+    pair_sum("st", part_t, acc_t, (5, 6))
     gather_step("c", call, 4)
-    backward(3)
     backward(4)
-    pair_sum("st", part_t, acc_t, (7, 5, 6))
+    ring_step(*mixed, 3)
+    pair_sum("st", part_t, acc_t, (7,))
     ring_start(*tgrad)
-    ring_step(*mixed, 3)
-    weight_terms(((2, 0), (2, 1), (0, 2), (1, 2)))
+    weight_terms(blocks[0], 7, 1)
     plane_far(0, 0)
     plane_far(1, 0)
-    ring_step(*tgrad, 3)
-    weight_terms(((2, 2), (2, 3), (3, 2), (1, 3)))
+    weight_terms(blocks[1], 7, 1)
     plane_far(0, 1)
     plane_far(1, 1)
     plane_near(0, 0)
-    ring_step(*mixed, 2)
-    weight_terms(((1, 0), (1, 1), (3, 0), (3, 1)))
+    weight_terms(blocks[2], 7, 1)
     plane_near(0, 1)
     plane_near(1, 0)
-    plane_chain(0, 0)
-    ring_step(*tgrad, 2)
-    weight_terms(((3, 3), (0, 1), (0, 3), (0, 0)))
+    weight_terms(blocks[3], 7, 1)
     plane_near(1, 1)
-    plane_chain(1, 0)
-    plane_chain(0, 1)
-    plane_chain(1, 1)
-    ring_step(*mixed, 1)
-    ring_step(*tgrad, 1)
+    for d in (0, 1):
+        for part in (0, 1):
+            plane_chain(part, d)
+    ring_step(*mixed, 2)
+    ring_step(*tgrad, 3)
     for s in range(8):
         for r in (0, 1):
             if s or r:
                 arrive(("g", s, r))
     grads = jnp.zeros((8, 128), F32)
-    lane = lax.broadcasted_iota(jnp.int32, (8, 128), 1)
     held = kept_ids[...]
     for s, o in enumerate(OFFSETS):
         for r in (0, 1):
@@ -373,20 +397,39 @@
                 tile = pltpu.roll(tile, 64, 1)
             grads = grads + jnp.where(held == hb[index_of(o, r)], tile, 0.0)
     gg_o[...] = grads[:, :64]
+    put(gg_o, gg_h)
+    ring_step(*mixed, 1)
+    ring_step(*tgrad, 2)
     plane_turn(0)
     plane_turn(1)
-    ring_end(*mixed, mixed_o)
     plane_chain2(0)
     plane_chain2(1)
     plane_end(0)
     plane_end(1)
-    ring_end(*tgrad, tg_o)
+    ring_step(*tgrad, 1)
     swap_relay(0)
     swap_relay(1)
+    ring_end(*mixed, mixed_o)
+    put(mixed_o, mixed_h)
+    ring_end(*tgrad, tg_o)
+    put(tg_o, tg_h)
     swap_end(0)
     swap_end(1)
+    put(wg_o, wg_h)
     for copy in copies.values():
         copy.wait_send()
+    for copy in outs:
+        copy.wait()
+
+
+def hand_on(*refs):
+    *pairs, sem = refs
+    half = len(pairs) // 2
+    copies = [pltpu.make_async_copy(a, b, sem.at[n]) for n, (a, b) in enumerate(zip(pairs[:half], pairs[half:]))]
+    for copy in copies:
+        copy.start()
+    for copy in copies:
+        copy.wait()
 
 
 COPIES = 240
@@ -422,26 +465,30 @@
         pltpu.VMEM((128, W3), BF16),
         pltpu.VMEM((128, W3), BF16),
         pltpu.VMEM((128, W3), BF16),
-        pltpu.VMEM((16, 8, 128), F32),
-        pltpu.VMEM((16, 8, 128), F32),
+        pltpu.VMEM((16, 16, 128), F32),
         pltpu.VMEM((rows, 128), F32),
         pltpu.VMEM((8, 8, 128), F32),
         pltpu.VMEM((16, 8, 128), F32),
         pltpu.VMEM((8, 128), jnp.int32),
+        pltpu.VMEM((TOK, D), BF16),
+        pltpu.VMEM((TOK, D), BF16),
+        pltpu.VMEM((8, TOK), F32),
+        pltpu.VMEM((3, 128, FF), F32),
         pltpu.SemaphoreType.DMA((COPIES,)),
         pltpu.SemaphoreType.DMA((COPIES,)),
-        pltpu.SemaphoreType.DMA((5,)),
+        pltpu.SemaphoreType.DMA((9,)),
     ]
-    mixed, token_grads, gate_grads, share = pl.pallas_call(
+    results = (
+        jax.ShapeDtypeStruct((TOK, D), BF16),
+        jax.ShapeDtypeStruct((TOK, D), BF16),
+        jax.ShapeDtypeStruct((8, TOK), F32),
+        jax.ShapeDtypeStruct((3, 128, FF), F32),
+    )
+    own = pl.pallas_call(
         kernel,
-        out_shape=(
-            jax.ShapeDtypeStruct((TOK, D), BF16),
-            jax.ShapeDtypeStruct((TOK, D), BF16),
-            jax.ShapeDtypeStruct((8, TOK), F32),
-            jax.ShapeDtypeStruct((3, 128, FF), F32),
-        ),
+        out_shape=results,
         in_specs=[smem, smem, vmem, vmem, anywhere, anywhere, anywhere],
-        out_specs=(vmem, vmem, vmem, vmem),
+        out_specs=(anywhere,) * 4,
         scratch_shapes=scratch,
         compiler_params=pltpu.CompilerParams(
             collective_id=0, has_side_effects=True, vmem_limit_bytes=62 * 1024 * 1024
@@ -455,6 +502,13 @@
         cotangent,
         jnp.transpose(weights[0], (1, 0, 2)),
     )
+    mixed, token_grads, gate_grads, share = pl.pallas_call(
+        hand_on,
+        out_shape=results,
+        in_specs=[anywhere] * 4,
+        out_specs=(anywhere,) * 4,
+        scratch_shapes=[pltpu.SemaphoreType.DMA((4,))],
+    )(*own)
     return mixed, token_grads, gate_grads.T, jnp.transpose(share, (1, 0, 2))[None]
 
 

time: 131 us -> 153 us (1.17)
  Pallas kernels: 124 us -> 151 us
  local copies, waits for them, and re-layouts: 6.53 us -> 0 us
    pallas_call x1 -> x2, Pallas kernels: 124 us -> 151 us  [the longest x1 116 us: on_device(): pl.pallas_call(kernel, out_shape=results, in_specs=[smem, smem, vmem, vme...]
    unnamed x4 -> x0, local copies, waits for them, and re-layouts: 6.53 us -> none
where the time goes in v2:
time: 153 us; the launch traced here: 152 us
  Pallas kernels  151 us (99%)
    pallas_call x1, Pallas kernels, on_device(): pl.pallas_call(kernel, out_shape=results, in_specs=[smem, smem, vmem, vme...  116 us
    pallas_call x1, Pallas kernels, on_device(): pl.pallas_call(hand_on, out_shape=results, in_specs=[anywhere] * 4, out_s...  35 us

profile of v2, /device:TPU:2, one launch (start us, length us, event | category | flops | bytes accessed | tf_op | source)
XLA Modules:
  0.0 151.9 jit_solution(4786921675930061251)
XLA Ops:
  0.6 116.1 %shard_map.102 = (bf16[64,2048]{1,0:T(8,128)(2,1)}, bf16[64,2048]{1,0:T(8,128)(2,1)}, f32[8,64]{1,0:T(8,128)}, f32[3,128,384]{2,1,0:T(8,128)}) custom-call(s32[16]{0:T(128)} %hb.1, s32[8]{0:T(128)} %flags.1, s32[8,64]{1,0:T(8,128)} %bitcast.10, f32[8,64]{1,0:T(8,128)} %bitcast.11, bf16[64,2048]{1,0:T(8,128)(2,1)} %tok.1, bf16[64,2048]{1,0:T(8,128)(2,1)} %cot.1, ...), custom_call_target="tpu_custom_call" | custom-call | tf_op jit(solution)/shard_map/pallas_call | solution.py:487
  116.7 35.0 %shard_map.103 = (bf16[64,2048]{1,0:T(8,128)(2,1)}, bf16[64,2048]{1,0:T(8,128)(2,1)}, f32[8,64]{1,0:T(8,128)}, f32[3,128,384]{2,1,0:T(8,128)}) custom-call(bf16[64,2048]{1,0:T(8,128)(2,1)} %get-tuple-element.12.refs_0_, bf16[64,2048]{1,0:T(8,128)(2,1)} %get-tuple-element.13.refs_1_, f32[8,64]{1,0:T(8,128)} %get-tuple-element.14.refs_2_, ...), custom_call_target="tpu_custom_call" | custom-call | tf_op jit(solution)/shard_map/pallas_call | solution.py:505

commit v3 on v2

--- a/solution.py
+++ b/solution.py
@@ -74,21 +74,24 @@
         copy.start()
     pl.semaphore_wait(barrier, len(peers))
 
-    def gather_own(name, src, dst):
-        for d, h in (("L", 0), ("R", 1), ("L", 1), ("R", 0)):
+    long, short = (("L", 0), ("R", 1)), (("L", 1), ("R", 0))
+
+    def gather_own(name, src, dst, pieces):
+        for d, h in pieces:
             step = 1 if d == "L" else -1
             send((name, d, 1, h), src.at[pl.ds(32 * h, 32)],
                  dst.at[pl.ds(row(SLOT[-step], 0, h), 32)], along_z(step))
+
+    def gather_pair(name, src, dst):
         send((name, "sib", 0), src, dst.at[pl.ds(64, 64)], along_z(0, 1))
 
     def gather_step(name, dst, s):
-        pieces = [("L", 0), ("R", 1)] + ([("L", 1), ("R", 0)] if s < 4 else [])
-        for d, h in pieces:
+        for d, h in long + short if s < 4 else long:
             step = 1 if d == "L" else -1
             slot = SLOT[-step * s]
             here = dst.at[pl.ds(row(slot, 0, h), 32)]
             arrive((name, d, s, h))
-            if s < 3 or (s == 3 and (d, h) in (("L", 0), ("R", 1))):
+            if s < 3 or (s == 3 and (d, h) in long):
                 there = dst.at[pl.ds(row(SLOT[-step * (s + 1)], 0, h), 32)]
                 send((name, d, s + 1, h), here, there, along_z(step))
             send((name, "sib", slot, h), here, dst.at[pl.ds(row(slot, 1, h), 32)], along_z(0, 1))
@@ -116,7 +119,8 @@
                 for h in (0, 1):
                     arrive((name, "sib", slot, h))
 
-    gather_own("x", tok, xall)
+    gather_own("x", tok, xall, long + short)
+    gather_pair("x", tok, xall)
 
     ids8, p8 = ids[...], probs[...]
     ids2 = jnp.concatenate([ids8, ids8], axis=1)
@@ -134,7 +138,7 @@
     kept = jnp.where(earlier < CAP - 0.5, 1.0, 0.0)
     wall[0] = jnp.concatenate(prob, axis=0) * kept
     weights_own()
-    gather_own("c", cot, call)
+    gather_own("c", cot, call, long)
     live = jnp.zeros((8, 128), F32)
     for j in range(16):
         live = live + jnp.where(ids2 == hb[j], jnp.broadcast_to(kept[j : j + 1], (8, 128)), 0.0)
@@ -334,56 +338,58 @@
         outs.append(copy)
 
     gather_step("x", xall, 1)
+    gather_own("c", cot, call, short)
     weights_step(1)
+    gather_pair("c", cot, call)
     forward(0)
+    forward(1)
+    gather_step("x", xall, 2)
     gather_step("c", call, 1)
-    gather_step("x", xall, 2)
     weights_step(2)
-    forward(1)
     backward(0)
     forward(2)
+    backward(1)
+    for some in blocks:
+        weight_terms(some, 0, 3)
+    pair_sum("sm", part_m, acc_m, (0, 1, 2, 3, 4))
+    gather_step("x", xall, 3)
     gather_step("c", call, 2)
-    gather_step("x", xall, 3)
     weights_step(3)
-    backward(1)
     forward(3)
     backward(2)
     for some in blocks:
-        weight_terms(some, 0, 3)
-    pair_sum("sm", part_m, acc_m, (0, 1, 2, 3, 4, 5, 6))
+        weight_terms(some, 3, 2)
+    pair_sum("sm", part_m, acc_m, (5, 6))
+    pair_sum("st", part_t, acc_t, (0, 1, 2, 3, 4))
+    gather_step("x", xall, 4)
     gather_step("c", call, 3)
-    gather_step("x", xall, 4)
     weights_step(4)
-    pair_sum("st", part_t, acc_t, (0, 1, 2, 3, 4))
     forward(4)
     pair_sum("sm", part_m, acc_m, (7,))
     ring_start(*mixed)
     backward(3)
-    for some in blocks:
-        weight_terms(some, 3, 4)
-    pair_sum("st", part_t, acc_t, (5, 6))
     gather_step("c", call, 4)
     backward(4)
     ring_step(*mixed, 3)
-    pair_sum("st", part_t, acc_t, (7,))
+    pair_sum("st", part_t, acc_t, (5, 6, 7))
     ring_start(*tgrad)
-    weight_terms(blocks[0], 7, 1)
+    weight_terms(blocks[0], 5, 3)
     plane_far(0, 0)
     plane_far(1, 0)
-    weight_terms(blocks[1], 7, 1)
+    weight_terms(blocks[1], 5, 3)
     plane_far(0, 1)
     plane_far(1, 1)
     plane_near(0, 0)
-    weight_terms(blocks[2], 7, 1)
+    weight_terms(blocks[2], 5, 3)
     plane_near(0, 1)
     plane_near(1, 0)
-    weight_terms(blocks[3], 7, 1)
+    weight_terms(blocks[3], 5, 3)
     plane_near(1, 1)
+    ring_step(*mixed, 2)
+    ring_step(*tgrad, 3)
     for d in (0, 1):
         for part in (0, 1):
             plane_chain(part, d)
-    ring_step(*mixed, 2)
-    ring_step(*tgrad, 3)
     for s in range(8):
         for r in (0, 1):
             if s or r:
@@ -423,13 +429,8 @@
 
 
 def hand_on(*refs):
-    *pairs, sem = refs
-    half = len(pairs) // 2
-    copies = [pltpu.make_async_copy(a, b, sem.at[n]) for n, (a, b) in enumerate(zip(pairs[:half], pairs[half:]))]
-    for copy in copies:
-        copy.start()
-    for copy in copies:
-        copy.wait()
+    for src, dst in zip(refs[:4], refs[4:]):
+        dst[...] = src[...]
 
 
 COPIES = 240
@@ -505,9 +506,8 @@
     mixed, token_grads, gate_grads, share = pl.pallas_call(
         hand_on,
         out_shape=results,
-        in_specs=[anywhere] * 4,
-        out_specs=(anywhere,) * 4,
-        scratch_shapes=[pltpu.SemaphoreType.DMA((4,))],
+        in_specs=[vmem] * 4,
+        out_specs=(vmem,) * 4,
     )(*own)
     return mixed, token_grads, gate_grads.T, jnp.transpose(share, (1, 0, 2))[None]
 

time: 153 us -> 116 us (0.76)
  Pallas kernels: 151 us -> 114 us
    pallas_call x1, Pallas kernels: 35 us -> 2.24 us  [on_device(): pl.pallas_call(hand_on, out_shape=results, in_specs=[vmem] * 4, out_specs...]
    pallas_call x1, Pallas kernels: 116 us -> 112 us  [on_device(): pl.pallas_call(kernel, out_shape=results, in_specs=[smem, smem, vmem, vme...]
where the time goes in v3:
time: 116 us; the launch traced here: 115 us
  Pallas kernels  114 us (98%)
    pallas_call x1, Pallas kernels, on_device(): pl.pallas_call(kernel, out_shape=results, in_specs=[smem, smem, vmem, vme...  112 us

profile of v3, /device:TPU:2, one launch (start us, length us, event | category | flops | bytes accessed | tf_op | source)
XLA Modules:
  0.0 114.9 jit_solution(7029679234517221216)
XLA Ops:
  0.6 112.0 %shard_map.102 = (bf16[64,2048]{1,0:T(8,128)(2,1)}, bf16[64,2048]{1,0:T(8,128)(2,1)}, f32[8,64]{1,0:T(8,128)}, f32[3,128,384]{2,1,0:T(8,128)}) custom-call(s32[16]{0:T(128)} %hb.1, s32[8]{0:T(128)} %flags.1, s32[8,64]{1,0:T(8,128)} %bitcast.10, f32[8,64]{1,0:T(8,128)} %bitcast.11, bf16[64,2048]{1,0:T(8,128)(2,1)} %tok.1, bf16[64,2048]{1,0:T(8,128)(2,1)} %cot.1, ...), custom_call_target="tpu_custom_call" | custom-call | tf_op jit(solution)/shard_map/pallas_call | solution.py:488
  112.7 2.2 %shard_map.103 = (bf16[64,2048]{1,0:T(8,128)(2,1)}, bf16[64,2048]{1,0:T(8,128)(2,1)}, f32[8,64]{1,0:T(8,128)}, f32[3,128,384]{2,1,0:T(8,128)}) custom-call(bf16[64,2048]{1,0:T(8,128)(2,1)} %get-tuple-element.12.refs_0_, bf16[64,2048]{1,0:T(8,128)(2,1)} %get-tuple-element.13.refs_1_, f32[8,64]{1,0:T(8,128)} %get-tuple-element.14.refs_2_, ...), custom_call_target="tpu_custom_call" | custom-call | tf_op jit(solution)/shard_map/pallas_call | solution.py:506

commit v4 on v3

--- a/solution.py
+++ b/solution.py
@@ -25,10 +25,10 @@
 
 def kernel(
     hb, flags, ids, probs, tok, cot, w,
-    mixed_h, tg_h, gg_h, wg_h,
+    mixed_o, tg_o, gg_o, wg_o,
     xall, call, w_in, w_d, up_slope, silu, hidden, whid, dgu, part_m, part_t, acc_m, acc_t,
     ring_m, ring_t, wg, r1, r2, red, q1, q2, share, relay, arrived,
-    wall, wcol, ggsend, ggrecv, kept_ids, mixed_o, tg_o, gg_o, wg_o,
+    wall, wcol, ggsend, ggrecv, kept_ids,
     send_sem, recv_sem, local_sem,
 ):
     px, py, e = lax.axis_index("dp_0"), lax.axis_index("dp_1"), lax.axis_index("expert")
@@ -85,8 +85,8 @@
     def gather_pair(name, src, dst):
         send((name, "sib", 0), src, dst.at[pl.ds(64, 64)], along_z(0, 1))
 
-    def gather_step(name, dst, s):
-        for d, h in long + short if s < 4 else long:
+    def gather_step(name, dst, s, pieces):
+        for d, h in pieces:
             step = 1 if d == "L" else -1
             slot = SLOT[-step * s]
             here = dst.at[pl.ds(row(slot, 0, h), 32)]
@@ -218,9 +218,9 @@
             slot = SLOT[k if d == 0 else -k]
             ring_send(name, acc, ring, d, k, h, acc.at[pl.ds(64 * slot + 32 * h, 32)])
 
-    def ring_step(name, acc, ring, k):
-        pieces = [(0, 0), (1, 1)] + ([(0, 1), (1, 0)] if k < 3 else [])
-        for d, h in pieces:
+    def ring_step(name, acc, ring, k, pieces):
+        for way, h in pieces:
+            d = 0 if way == "L" else 1
             arrive((name, d, k, h))
             slot = SLOT[k if d == 0 else -k]
             there = pl.ds(64 * k + 32 * h, 32)
@@ -330,21 +330,14 @@
         ((1, 0), (1, 1), (3, 0), (3, 1)),
         ((3, 3), (0, 1), (0, 3), (0, 0)),
     )
-    outs = []
-
-    def put(src, dst):
-        copy = pltpu.make_async_copy(src, dst, local_sem.at[5 + len(outs)])
-        copy.start()
-        outs.append(copy)
-
-    gather_step("x", xall, 1)
+    gather_step("x", xall, 1, long + short)
     gather_own("c", cot, call, short)
     weights_step(1)
     gather_pair("c", cot, call)
     forward(0)
     forward(1)
-    gather_step("x", xall, 2)
-    gather_step("c", call, 1)
+    gather_step("x", xall, 2, long + short)
+    gather_step("c", call, 1, long + short)
     weights_step(2)
     backward(0)
     forward(2)
@@ -352,8 +345,8 @@
     for some in blocks:
         weight_terms(some, 0, 3)
     pair_sum("sm", part_m, acc_m, (0, 1, 2, 3, 4))
-    gather_step("x", xall, 3)
-    gather_step("c", call, 2)
+    gather_step("x", xall, 3, long + short)
+    gather_step("c", call, 2, long + short)
     weights_step(3)
     forward(3)
     backward(2)
@@ -361,18 +354,16 @@
         weight_terms(some, 3, 2)
     pair_sum("sm", part_m, acc_m, (5, 6))
     pair_sum("st", part_t, acc_t, (0, 1, 2, 3, 4))
-    gather_step("x", xall, 4)
-    gather_step("c", call, 3)
+    gather_step("x", xall, 4, long)
+    gather_step("c", call, 3, long + short)
     weights_step(4)
     forward(4)
     pair_sum("sm", part_m, acc_m, (7,))
     ring_start(*mixed)
     backward(3)
-    gather_step("c", call, 4)
+    gather_step("c", call, 4, long)
     backward(4)
-    ring_step(*mixed, 3)
-    pair_sum("st", part_t, acc_t, (5, 6, 7))
-    ring_start(*tgrad)
+    ring_step(*mixed, 3, long)
     weight_terms(blocks[0], 5, 3)
     plane_far(0, 0)
     plane_far(1, 0)
@@ -380,16 +371,29 @@
     plane_far(0, 1)
     plane_far(1, 1)
     plane_near(0, 0)
+    pair_sum("st", part_t, acc_t, (5, 6, 7))
+    ring_start(*tgrad)
     weight_terms(blocks[2], 5, 3)
     plane_near(0, 1)
     plane_near(1, 0)
     weight_terms(blocks[3], 5, 3)
     plane_near(1, 1)
-    ring_step(*mixed, 2)
-    ring_step(*tgrad, 3)
+    ring_step(*mixed, 2, long + short)
     for d in (0, 1):
         for part in (0, 1):
             plane_chain(part, d)
+    ring_step(*tgrad, 3, long)
+    ring_step(*mixed, 1, long + short)
+    ring_step(*tgrad, 2, long + short)
+    plane_turn(0)
+    plane_turn(1)
+    plane_chain2(0)
+    plane_chain2(1)
+    plane_end(0)
+    plane_end(1)
+    ring_step(*tgrad, 1, long + short)
+    swap_relay(0)
+    swap_relay(1)
     for s in range(8):
         for r in (0, 1):
             if s or r:
@@ -403,34 +407,21 @@
                 tile = pltpu.roll(tile, 64, 1)
             grads = grads + jnp.where(held == hb[index_of(o, r)], tile, 0.0)
     gg_o[...] = grads[:, :64]
-    put(gg_o, gg_h)
-    ring_step(*mixed, 1)
-    ring_step(*tgrad, 2)
-    plane_turn(0)
-    plane_turn(1)
-    plane_chain2(0)
-    plane_chain2(1)
-    plane_end(0)
-    plane_end(1)
-    ring_step(*tgrad, 1)
-    swap_relay(0)
-    swap_relay(1)
     ring_end(*mixed, mixed_o)
-    put(mixed_o, mixed_h)
     ring_end(*tgrad, tg_o)
-    put(tg_o, tg_h)
     swap_end(0)
     swap_end(1)
-    put(wg_o, wg_h)
     for copy in copies.values():
         copy.wait_send()
-    for copy in outs:
+
+
+def hand_on(*refs):
+    *refs, sem = refs
+    copies = [pltpu.make_async_copy(refs[n], refs[4 + n], sem.at[n]) for n in range(4)]
+    for copy in copies:
+        copy.start()
+    for copy in copies:
         copy.wait()
-
-
-def hand_on(*refs):
-    for src, dst in zip(refs[:4], refs[4:]):
-        dst[...] = src[...]
 
 
 COPIES = 240
@@ -471,13 +462,9 @@
         pltpu.VMEM((8, 8, 128), F32),
         pltpu.VMEM((16, 8, 128), F32),
         pltpu.VMEM((8, 128), jnp.int32),
-        pltpu.VMEM((TOK, D), BF16),
-        pltpu.VMEM((TOK, D), BF16),
-        pltpu.VMEM((8, TOK), F32),
-        pltpu.VMEM((3, 128, FF), F32),
         pltpu.SemaphoreType.DMA((COPIES,)),
         pltpu.SemaphoreType.DMA((COPIES,)),
-        pltpu.SemaphoreType.DMA((9,)),
+        pltpu.SemaphoreType.DMA((5,)),
     ]
     results = (
         jax.ShapeDtypeStruct((TOK, D), BF16),
@@ -487,9 +474,9 @@
     )
     own = pl.pallas_call(
         kernel,
-        out_shape=results,
+        out_shape=tuple(pltpu.VMEM(r.shape, r.dtype) for r in results),
         in_specs=[smem, smem, vmem, vmem, anywhere, anywhere, anywhere],
-        out_specs=(anywhere,) * 4,
+        out_specs=(vmem,) * 4,
         scratch_shapes=scratch,
         compiler_params=pltpu.CompilerParams(
             collective_id=0, has_side_effects=True, vmem_limit_bytes=62 * 1024 * 1024
@@ -503,11 +490,13 @@
         cotangent,
         jnp.transpose(weights[0], (1, 0, 2)),
     )
+    own = [pltpu.with_memory_space_constraint(x, pltpu.VMEM) for x in own]
     mixed, token_grads, gate_grads, share = pl.pallas_call(
         hand_on,
         out_shape=results,
         in_specs=[vmem] * 4,
-        out_specs=(vmem,) * 4,
+        out_specs=(anywhere,) * 4,
+        scratch_shapes=[pltpu.SemaphoreType.DMA((4,))],
     )(*own)
     return mixed, token_grads, gate_grads.T, jnp.transpose(share, (1, 0, 2))[None]
 

time: 116 us -> 114 us (0.983)
  Pallas kernels: 114 us -> 112 us
    pallas_call x1, Pallas kernels: 112 us -> 111 us  [on_device(): pl.pallas_call(kernel, out_shape=tuple((pltpu.VMEM(r.shape, r.dtype) for...]
    pallas_call x1, Pallas kernels: 2.24 us -> 1.03 us  [on_device(): pl.pallas_call(hand_on, out_shape=results, in_specs=[vmem] * 4, out_specs...]
where the time goes in v4:
time: 114 us; the launch traced here: 112 us
  Pallas kernels  112 us (98%)
    pallas_call x1, Pallas kernels, on_device(): pl.pallas_call(kernel, out_shape=tuple((pltpu.VMEM(r.shape, r.dtype) for...  111 us

profile of v4, /device:TPU:2, one launch (start us, length us, event | category | flops | bytes accessed | tf_op | source)
XLA Modules:
  0.0 112.4 jit_solution(17008956924524938414)
XLA Ops:
  0.6 110.6 %shard_map.102 = (bf16[64,2048]{1,0:T(8,128)(2,1)S(1)}, bf16[64,2048]{1,0:T(8,128)(2,1)S(1)}, f32[8,64]{1,0:T(8,128)S(1)}, f32[3,128,384]{2,1,0:T(8,128)S(1)}) custom-call(s32[16]{0:T(128)} %hb.1, s32[8]{0:T(128)} %flags.1, s32[8,64]{1,0:T(8,128)} %bitcast.10, f32[8,64]{1,0:T(8,128)} %bitcast.11, bf16[64,2048]{1,0:T(8,128)(2,1)} %tok.1, ...), custom_call_target="tpu_custom_call" | custom-call | tf_op jit(solution)/shard_map/pallas_call | solution.py:475
  111.2 1.0 shard_map.103

commit v5 on v4

--- a/solution.py
+++ b/solution.py
@@ -213,8 +213,10 @@
         step = 1 if d == 0 else -1
         send((name, d, k - 1, h), src, ring.at[d, pl.ds(64 * (k - 1) + 32 * h, 32)], along_z(step))
 
-    def ring_start(name, acc, ring):
-        for d, k, h in ((0, 4, 0), (1, 4, 1), (0, 3, 1), (1, 3, 0)):
+    def ring_start(name, acc, ring, pieces):
+        k = 4 if pieces == long else 3
+        for way, h in pieces:
+            d = 0 if way == "L" else 1
             slot = SLOT[k if d == 0 else -k]
             ring_send(name, acc, ring, d, k, h, acc.at[pl.ds(64 * slot + 32 * h, 32)])
 
@@ -358,12 +360,12 @@
     gather_step("c", call, 3, long + short)
     weights_step(4)
     forward(4)
+    ring_start(*mixed, short)
+    backward(3)
     pair_sum("sm", part_m, acc_m, (7,))
-    ring_start(*mixed)
-    backward(3)
+    ring_start(*mixed, long)
     gather_step("c", call, 4, long)
     backward(4)
-    ring_step(*mixed, 3, long)
     weight_terms(blocks[0], 5, 3)
     plane_far(0, 0)
     plane_far(1, 0)
@@ -371,8 +373,10 @@
     plane_far(0, 1)
     plane_far(1, 1)
     plane_near(0, 0)
+    ring_step(*mixed, 3, long)
     pair_sum("st", part_t, acc_t, (5, 6, 7))
-    ring_start(*tgrad)
+    ring_start(*tgrad, long)
+    ring_start(*tgrad, short)
     weight_terms(blocks[2], 5, 3)
     plane_near(0, 1)
     plane_near(1, 0)

time: 114 us -> 114 us (level); the launches traced: 112 us -> 114 us
    pallas_call x1, Pallas kernels: 111 us -> 112 us  [on_device(): pl.pallas_call(kernel, out_shape=tuple((pltpu.VMEM(r.shape, r.dtype) for...]
where the time goes in v5:
time: 114 us
  Pallas kernels  113 us (99%)
    pallas_call x1, Pallas kernels, on_device(): pl.pallas_call(kernel, out_shape=tuple((pltpu.VMEM(r.shape, r.dtype) for...  112 us

profile of v5, /device:TPU:2, one launch (start us, length us, event | category | flops | bytes accessed | tf_op | source)
XLA Modules:
  0.0 114.1 jit_solution(441798037506590949)
XLA Ops:
  0.6 112.2 %shard_map.102 = (bf16[64,2048]{1,0:T(8,128)(2,1)S(1)}, bf16[64,2048]{1,0:T(8,128)(2,1)S(1)}, f32[8,64]{1,0:T(8,128)S(1)}, f32[3,128,384]{2,1,0:T(8,128)S(1)}) custom-call(s32[16]{0:T(128)} %hb.1, s32[8]{0:T(128)} %flags.1, s32[8,64]{1,0:T(8,128)} %bitcast.10, f32[8,64]{1,0:T(8,128)} %bitcast.11, bf16[64,2048]{1,0:T(8,128)(2,1)} %tok.1, ...), custom_call_target="tpu_custom_call" | custom-call | tf_op jit(solution)/shard_map/pallas_call | solution.py:479
  112.9 1.0 shard_map.103

commit v6 on v4

--- a/solution.py
+++ b/solution.py
@@ -358,12 +358,11 @@
     gather_step("c", call, 3, long + short)
     weights_step(4)
     forward(4)
+    backward(3)
     pair_sum("sm", part_m, acc_m, (7,))
     ring_start(*mixed)
-    backward(3)
     gather_step("c", call, 4, long)
     backward(4)
-    ring_step(*mixed, 3, long)
     weight_terms(blocks[0], 5, 3)
     plane_far(0, 0)
     plane_far(1, 0)
@@ -371,6 +370,7 @@
     plane_far(0, 1)
     plane_far(1, 1)
     plane_near(0, 0)
+    ring_step(*mixed, 3, long)
     pair_sum("st", part_t, acc_t, (5, 6, 7))
     ring_start(*tgrad)
     weight_terms(blocks[2], 5, 3)
@@ -378,15 +378,15 @@
     plane_near(1, 0)
     weight_terms(blocks[3], 5, 3)
     plane_near(1, 1)
-    ring_step(*mixed, 2, long + short)
     for d in (0, 1):
         for part in (0, 1):
             plane_chain(part, d)
+    ring_step(*mixed, 2, long + short)
     ring_step(*tgrad, 3, long)
     ring_step(*mixed, 1, long + short)
-    ring_step(*tgrad, 2, long + short)
     plane_turn(0)
     plane_turn(1)
+    ring_step(*tgrad, 2, long + short)
     plane_chain2(0)
     plane_chain2(1)
     plane_end(0)

time: 114 us -> 114 us (level)
  no operation moved by 1% of the time
where the time goes in v6:
time: 114 us
  Pallas kernels  113 us (99%)
    pallas_call x1, Pallas kernels, on_device(): pl.pallas_call(kernel, out_shape=tuple((pltpu.VMEM(r.shape, r.dtype) for...  112 us

profile of v6, /device:TPU:2, one launch (start us, length us, event | category | flops | bytes accessed | tf_op | source)
XLA Modules:
  0.0 113.5 jit_solution(10867513924815595606)
XLA Ops:
  0.6 111.7 %shard_map.102 = (bf16[64,2048]{1,0:T(8,128)(2,1)S(1)}, bf16[64,2048]{1,0:T(8,128)(2,1)S(1)}, f32[8,64]{1,0:T(8,128)S(1)}, f32[3,128,384]{2,1,0:T(8,128)S(1)}) custom-call(s32[16]{0:T(128)} %hb.1, s32[8]{0:T(128)} %flags.1, s32[8,64]{1,0:T(8,128)} %bitcast.10, f32[8,64]{1,0:T(8,128)} %bitcast.11, bf16[64,2048]{1,0:T(8,128)(2,1)} %tok.1, ...), custom_call_target="tpu_custom_call" | custom-call | tf_op jit(solution)/shard_map/pallas_call | solution.py:475
  112.3 1.0 shard_map.103
